TPU v7x, 256 devices: a whole 4x4x8 slice. The times are simulated.
256 devices in a mesh: gx: 16 (over z, core), gy: 16 (over x, y).
Axes of the slice: x: 4, y: 4, z: 8, core: 2. Of those that a mesh axis runs over, the one named last changes fastest.
Arguments:
- gradient: float32 [3, 128, 128, 256], P(None, 'gx', 'gy'), may hold values from -80 to 80
- potential: float32 [128, 128, 256], P('gx', 'gy'), may hold values from -6 to 6
- coupling: float32 [3, 3, 128, 128, 256], P(None, None, 'gx', 'gy'), may hold values from -1 to 1
- region: int32 [128, 128, 256], P('gx', 'gy'), may hold values from 0 to 3
- contact: int32 [128, 128, 256], P('gx', 'gy'), may hold values 0 or 1
- rates: float32 [4, 3], replicated, may hold values from 3.5 to 10
Outputs:
- adjoint: float32 [3, 128, 128, 256], P(None, 'gx', 'gy')
All inputs are finite; a program needn't handle non-finite values. No bound on the sum of `contact` on one device may be relied on, other than what follows from the above.
Results may differ from a plain program's by a relative error of at most 0.0003.
Values sent between devices are 32-bit elements; how exact they have to be, the bound alone decides.
A program may use at most 192 MiB of HBM per device.

v0:
```python
import jax
import jax.numpy as jnp
from jax import lax
from jax.sharding import PartitionSpec as P

LEVELS = 4
COARSE_SWEEPS = 6
REGIONS = 4


OMEGA = 0.8
STRENGTH = 8.0


def padded_2(block, sides, width):
    for axis, dim in sides:
        count = lax.axis_size(axis)
        forward = [(i, i + 1) for i in range(count - 1)]
        backward = [(target, source) for source, target in forward]
        low = lax.ppermute(
            lax.slice_in_dim(block, block.shape[dim] - width, None, axis=dim), axis, forward
        )
        high = lax.ppermute(lax.slice_in_dim(block, 0, width, axis=dim), axis, backward)
        block = jnp.concatenate([low, block, high], axis=dim)
    return block


def bernoulli(value):
    is_small = jnp.abs(value) < 0.0001
    safe_arg = jnp.where(is_small, 1.0, value)
    return jnp.where(is_small, 1.0 - 0.5 * value, safe_arg / jnp.expm1(safe_arg))


def beside_cells(padded):
    return [
        padded[..., 2:, 1:-1, 1:-1],
        padded[..., :-2, 1:-1, 1:-1],
        padded[..., 1:-1, 2:, 1:-1],
        padded[..., 1:-1, :-2, 1:-1],
        padded[..., 1:-1, 1:-1, 2:],
        padded[..., 1:-1, 1:-1, :-2],
    ]


def outgoing_weights(potential, padded):
    unity = jnp.ones_like(potential)
    stacked = []
    for beside in beside_cells(padded):
        difference = potential - beside
        stacked.append(jnp.stack([unity, bernoulli(difference), bernoulli(-difference)]))
    return jnp.stack(stacked)


def node_reaction(coupling, region, contact, rates):
    contact_value = contact.astype(coupling.dtype)
    rows_list = []
    for component in range(3):
        diagonal_extra = STRENGTH * contact_value
        for region_pick in range(REGIONS):
            diagonal_extra = diagonal_extra + jnp.where(
                region == region_pick, rates[region_pick, component], 0.0
            )
        rows_list.append(diagonal_extra)
    diagonal = jnp.stack(rows_list)
    identity = jnp.eye(3, dtype=coupling.dtype)[:, :, None, None, None]
    return coupling + identity * diagonal[:, None]


def cofactor_entry(entries, row_pick, col_pick):
    row_one, row_two = ((row_pick + 1) % 3, (row_pick + 2) % 3)
    col_one, col_two = ((col_pick + 1) % 3, (col_pick + 2) % 3)
    return (
        entries[row_one][col_one] * entries[row_two][col_two]
        - entries[row_one][col_two] * entries[row_two][col_one]
    )


def diag_inverse(weights, reaction):
    sums = jnp.sum(weights, axis=0)
    entries = [
        [
            reaction[col_pick, row_pick] + (sums[row_pick] if row_pick == col_pick else 0.0)
            for col_pick in range(3)
        ]
        for row_pick in range(3)
    ]
    cofactor = [
        [cofactor_entry(entries, row_pick, col_pick) for col_pick in range(3)]
        for row_pick in range(3)
    ]
    determinant = (
        entries[0][0] * cofactor[0][0]
        + entries[0][1] * cofactor[0][1]
        + entries[0][2] * cofactor[0][2]
    )
    return jnp.stack(
        [
            jnp.stack([cofactor[col_pick][row_pick] / determinant for col_pick in range(3)])
            for row_pick in range(3)
        ]
    )


def apply_inverse(inverse, residual):
    return jnp.sum(inverse * residual[None], axis=1)


def apply_adjoint(field, padded, weights, reaction):
    total = jnp.sum(weights, axis=0) * field
    for direction, beside in enumerate(beside_cells(padded)):
        total = total - weights[direction] * beside
    return total + jnp.sum(reaction * field[:, None], axis=0)


def coarsen_level(weights, reaction):
    span_x, span_y, span_z = (weights.shape[2], weights.shape[3], weights.shape[4])
    blocks = weights.reshape(6, 3, span_x // 2, 2, span_y // 2, 2, span_z // 2, 2)
    picks = [(2, 1), (2, 0), (4, 1), (4, 0), (6, 1), (6, 0)]
    coarse_weights = jnp.stack(
        [
            jnp.sum(
                lax.index_in_dim(blocks[direction], face_side, sub_axis, keepdims=True),
                axis=(2, 4, 6),
            )
            for direction, (sub_axis, face_side) in enumerate(picks)
        ]
    )
    coarse_reaction = jnp.sum(
        reaction.reshape(3, 3, span_x // 2, 2, span_y // 2, 2, span_z // 2, 2), axis=(3, 5, 7)
    )
    return (coarse_weights, coarse_reaction)


def restrict_field(field):
    span_x, span_y, span_z = (field.shape[1], field.shape[2], field.shape[3])
    return jnp.sum(field.reshape(3, span_x // 2, 2, span_y // 2, 2, span_z // 2, 2), axis=(2, 4, 6))


def prolong_field(field):
    span_x, span_y, span_z = (field.shape[1], field.shape[2], field.shape[3])
    spread = jnp.broadcast_to(
        field[:, :, None, :, None, :, None], (3, span_x, 2, span_y, 2, span_z, 2)
    )
    return spread.reshape(3, 2 * span_x, 2 * span_y, 2 * span_z)


def padded_field(field):
    extended = padded_2(field, (("gx", 1), ("gy", 2)), 1)
    return jnp.pad(extended, ((0, 0), (0, 0), (0, 0), (1, 1)))


def smooth_sweep(source, current, weights, reaction, inverse):
    residual = source - apply_adjoint(current, padded_field(current), weights, reaction)
    return current + OMEGA * apply_inverse(inverse, residual)


def coarse_solve(source, coarse_data):
    weights, reaction, inverse = coarse_data
    current = OMEGA * apply_inverse(inverse, source)
    for sweep_index in range(COARSE_SWEEPS - 1):
        current = smooth_sweep(source, current, weights, reaction, inverse)
    return current


def multigrid_cycle(level_index, source, current, from_zero, levels, coarse_data, grown_data):
    if level_index == LEVELS - 1:
        return coarse_solve(source, coarse_data)
    weights, reaction, inverse = levels[level_index]
    if from_zero:
        current = OMEGA * apply_inverse(inverse, source)
        residual = source - apply_adjoint(current, padded_field(current), weights, reaction)
    else:
        current = smooth_sweep(source, current, weights, reaction, inverse)
        residual = source - apply_adjoint(current, padded_field(current), weights, reaction)
    correction = multigrid_cycle(
        level_index + 1, restrict_field(residual), None, True, levels, coarse_data, grown_data
    )
    current = current + prolong_field(correction)
    return smooth_sweep(source, current, weights, reaction, inverse)


def local(gradient, potential, coupling, region, contact, rates):
    rim_width = 1
    extended = padded_2(potential, (("gx", 0), ("gy", 1)), rim_width)
    padded_potential = jnp.pad(extended, ((0, 0), (0, 0), (1, 1)))
    reaction = node_reaction(coupling, region, contact, rates)
    grown_data = None
    weights = outgoing_weights(potential, padded_potential)
    levels = [(weights, reaction, diag_inverse(weights, reaction))]
    for level_index in range(1, LEVELS):
        coarse_weights, coarse_reaction = coarsen_level(levels[-1][0], levels[-1][1])
        levels.append(
            (coarse_weights, coarse_reaction, diag_inverse(coarse_weights, coarse_reaction))
        )
    coarse_data = levels[-1]
    adjoint = multigrid_cycle(0, gradient, None, True, levels, coarse_data, grown_data)
    adjoint = multigrid_cycle(0, gradient, adjoint, False, levels, coarse_data, grown_data)
    return adjoint


def solution(mesh):
    placed = (
        P(None, "gx", "gy", None),
        P("gx", "gy", None),
        P(None, None, "gx", "gy", None),
        P("gx", "gy", None),
        P("gx", "gy", None),
        P(),
    )
    return jax.shard_map(
        local, mesh=mesh, in_specs=placed, out_specs=P(None, "gx", "gy", None), check_vma=False
    )
```

profile of v0, /device:TPU:134, one launch (start us, length us, event | category | flops | bytes accessed | tf_op | source)
XLA Modules:
  0.0 779.1 jit_solution(720174332163855768)
XLA Ops:
  10.4 5.9 add_bitcast_fusion.1
  17.6 39.1 %reshape.2949 = f32[3,3,4,2,4,2,128,2]{7,6,5,4,3,2,1,0:T(8,128)} reshape(f32[3,3,8,8,256]{4,3,2,1,0:T(8,128)S(1)} %multiply_add_fusion) | data formatting | bytes 1179648 | tf_op jit(solution)/shard_map/reshape | solution.py:129
  56.7 13.7 %reduce_sum.1153 = f32[3,3,4,4,128]{4,3,2,1,0:T(4,128)S(1)} reduce(f32[3,3,4,2,4,2,128,2]{7,6,5,4,3,2,1,0:T(8,128)} %reshape.2949, f32[]{:T(128)} %constant.12.clone.1), dimensions={3,5,7}, to_apply=%region_1.2 | reduce | flops 129024 | bytes 663556 | tf_op jit(solution)/shard_map/reduce_sum | solution.py:128
  70.4 6.2 reshape.2951
  80.9 5.2 collective-permute-start.2
  88.2 5.5 stack.286
  96.5 5.5 stack.285
  104.9 5.5 stack.283
  113.2 5.5 stack.282
  133.7 5.5 stack.295
  139.2 6.0 stack.294
  145.2 5.5 stack.298
  150.7 5.5 stack.297
  156.2 5.5 stack.289
  161.7 5.5 stack.288
  167.2 5.6 stack.292
  172.8 5.5 stack.291
  254.6 5.8 collective-permute-start.6
  262.8 5.4 collective-permute-done.7
  270.7 14.7 %reshape.2950 = f32[3,4,2,4,2,128,2]{6,5,4,3,2,1,0:T(8,128)} reshape(f32[3,8,8,256]{3,2,1,0:T(8,128)} %fusion.52) | data formatting | bytes 393216 | tf_op jit(solution)/shard_map/reshape | solution.py:136
  285.4 5.5 reduce_sum.1166
  336.1 4.9 collective-permute-start.16
  358.3 4.2 collective-permute-done.21
  469.6 5.1 broadcast_in_dim.175
  474.8 10.0 %reshape.2954 = f32[3,8,8,256]{3,2,1,0:T(8,128)S(1)} reshape(f32[3,4,2,4,2,128,2]{6,5,4,3,2,1,0:T(8,128)} %broadcast_in_dim.175) | data formatting | bytes 393216 | tf_op jit(solution)/shard_map/reshape | solution.py:144
  533.4 4.2 collective-permute-start.55
  542.1 13.9 %reshape.2955 = f32[3,4,2,4,2,128,2]{6,5,4,3,2,1,0:T(8,128)} reshape(f32[3,8,8,256]{3,2,1,0:T(8,128)S(1)} %fusion.16) | data formatting | bytes 393216 | tf_op jit(solution)/shard_map/reshape | solution.py:136
  556.1 5.6 reduce_sum.1238
  605.9 4.9 collective-permute-start.64
  628.8 4.2 collective-permute-done.69
  743.5 5.1 broadcast_in_dim.180
  748.7 9.9 %reshape.2958 = f32[3,8,8,256]{3,2,1,0:T(8,128)S(1)} reshape(f32[3,4,2,4,2,128,2]{6,5,4,3,2,1,0:T(8,128)} %broadcast_in_dim.180) | data formatting | bytes 393216 | tf_op jit(solution)/shard_map/reshape | solution.py:144
  (666 shorter events, 535.3 us)
Async XLA Ops:
  0.7 79.3 %collective-permute-start = (f32[1,8,256]{2,1,0:T(8,128)S(1)}, f32[1,8,256]{2,1,0:T(8,128)S(1)}, u32[]{:S(2)}, u32[]{:S(2)}) collective-permute-start(f32[1,8,256]{2,1,0:T(8,128)S(1)} %get-tuple-element.118), channel_id=1, source_target_pairs={{16,0},{32,16},{48,32},{64,48},{80,64},{96,80},{112,96},{128,112},... | collective-permute-start | bytes 24584 | tf_op jit(solution)/shard_map/ppermute | solution.py:23
  2.6 77.3 %collective-permute-start.1 = (f32[1,8,256]{2,1,0:T(8,128)S(1)}, f32[1,8,256]{2,1,0:T(8,128)S(1)}, u32[]{:S(2)}, u32[]{:S(2)}) collective-permute-start(f32[1,8,256]{2,1,0:T(8,128)S(1)} %get-tuple-element.119), channel_id=1, source_target_pairs={{0,16},{16,32},{32,48},{48,64},{64,80},{80,96},{96,112},{112,128},... | collective-permute-start | bytes 24584 | tf_op jit(solution)/shard_map/ppermute | solution.py:20
  80.9 48.3 %collective-permute-start.2 = (f32[10,1,256]{2,1,0:T(1,128)}, f32[10,1,256]{2,1,0:T(1,128)}, u32[]{:S(2)}, u32[]{:S(2)}) collective-permute-start(f32[10,1,256]{2,1,0:T(1,128)} %get-tuple-element.104), channel_id=1, source_target_pairs={{1,0},{2,1},{3,2},{4,3},{5,4},{6,5},{7,6},{8,7},{9,8},{10,9},{11,1... | collective-permute-start | bytes 30728 | tf_op jit(solution)/shard_map/ppermute | solution.py:23
  86.0 43.1 %collective-permute-start.3 = (f32[10,1,256]{2,1,0:T(1,128)}, f32[10,1,256]{2,1,0:T(1,128)}, u32[]{:S(2)}, u32[]{:S(2)}) collective-permute-start(f32[10,1,256]{2,1,0:T(1,128)} %get-tuple-element.103), channel_id=1, source_target_pairs={{0,1},{1,2},{2,3},{3,4},{4,5},{5,6},{6,7},{7,8},{8,9},{9,10},{10,1... | collective-permute-start | bytes 30728 | tf_op jit(solution)/shard_map/ppermute | solution.py:20
  230.1 24.4 %collective-permute-start.4 = (f32[3,1,8,256]{3,2,1,0:T(8,128)}, f32[3,1,8,256]{3,2,1,0:T(8,128)S(1)}, u32[]{:S(2)}, u32[]{:S(2)}) collective-permute-start(f32[3,1,8,256]{3,2,1,0:T(8,128)} %get-tuple-element.89), channel_id=1, source_target_pairs={{16,0},{32,16},{48,32},{64,48},{80,64},{96,80},{112,96},{128,112},... | collective-permute-start | bytes 73736 | tf_op jit(solution)/shard_map/ppermute | solution.py:23
  234.2 20.4 %collective-permute-start.5 = (f32[3,1,8,256]{3,2,1,0:T(8,128)}, f32[3,1,8,256]{3,2,1,0:T(8,128)S(1)}, u32[]{:S(2)}, u32[]{:S(2)}) collective-permute-start(f32[3,1,8,256]{3,2,1,0:T(8,128)} %get-tuple-element.88), channel_id=1, source_target_pairs={{0,16},{16,32},{32,48},{48,64},{64,80},{80,96},{96,112},{112,128},... | collective-permute-start | bytes 73736 | tf_op jit(solution)/shard_map/ppermute | solution.py:20
  254.6 8.3 %collective-permute-start.6 = (f32[3,10,1,256]{3,2,1,0:T(1,128)S(1)}, f32[3,10,1,256]{3,2,1,0:T(1,128)S(1)}, u32[]{:S(2)}, u32[]{:S(2)}) collective-permute-start(f32[3,10,1,256]{3,2,1,0:T(1,128)S(1)} %get-tuple-element.79), channel_id=1, source_target_pairs={{1,0},{2,1},{3,2},{4,3},{5,4},{6,5},{7,6},{8,7},{9,8},{10,9},{11,1... | collective-permute-start | bytes 92168 | tf_op jit(solution)/shard_map/ppermute | solution.py:23
  260.3 7.9 %collective-permute-start.7 = (f32[3,10,1,256]{3,2,1,0:T(1,128)S(1)}, f32[3,10,1,256]{3,2,1,0:T(1,128)S(1)}, u32[]{:S(2)}, u32[]{:S(2)}) collective-permute-start(f32[3,10,1,256]{3,2,1,0:T(1,128)S(1)} %get-tuple-element.78), channel_id=1, source_target_pairs={{0,1},{1,2},{2,3},{3,4},{4,5},{5,6},{6,7},{7,8},{8,9},{9,10},{10,1... | collective-permute-start | bytes 92168 | tf_op jit(solution)/shard_map/ppermute | solution.py:20
  302.6 7.7 collective-permute-start.11
  324.6 7.6 collective-permute-start.15
  334.1 6.8 collective-permute-start.17
  344.1 7.6 collective-permute-start.19
  364.5 7.6 collective-permute-start.23
  383.0 7.6 collective-permute-start.27
  401.6 7.6 collective-permute-start.31
  420.1 7.6 collective-permute-start.35
  438.9 7.6 collective-permute-start.39
  460.0 7.7 collective-permute-start.43
  495.1 7.9 %collective-permute-start.47 = (f32[3,10,1,256]{3,2,1,0:T(1,128)S(1)}, f32[3,10,1,256]{3,2,1,0:T(1,128)S(1)}, u32[]{:S(2)}, u32[]{:S(2)}) collective-permute-start(f32[3,10,1,256]{3,2,1,0:T(1,128)S(1)} %get-tuple-element.76), channel_id=1, source_target_pairs={{0,1},{1,2},{2,3},{3,4},{4,5},{5,6},{6,7},{7,8},{8,9},{9,10},{10,1... | collective-permute-start | bytes 92168 | tf_op jit(solution)/shard_map/ppermute | solution.py:20
  514.4 7.9 %collective-permute-start.51 = (f32[3,10,1,256]{3,2,1,0:T(1,128)S(1)}, f32[3,10,1,256]{3,2,1,0:T(1,128)S(1)}, u32[]{:S(2)}, u32[]{:S(2)}) collective-permute-start(f32[3,10,1,256]{3,2,1,0:T(1,128)S(1)} %get-tuple-element.74), channel_id=1, source_target_pairs={{0,1},{1,2},{2,3},{3,4},{4,5},{5,6},{6,7},{7,8},{8,9},{9,10},{10,1... | collective-permute-start | bytes 92168 | tf_op jit(solution)/shard_map/ppermute | solution.py:20
  533.4 7.9 %collective-permute-start.55 = (f32[3,10,1,256]{3,2,1,0:T(1,128)S(1)}, f32[3,10,1,256]{3,2,1,0:T(1,128)S(1)}, u32[]{:S(2)}, u32[]{:S(2)}) collective-permute-start(f32[3,10,1,256]{3,2,1,0:T(1,128)S(1)} %get-tuple-element.72), channel_id=1, source_target_pairs={{0,1},{1,2},{2,3},{3,4},{4,5},{5,6},{6,7},{7,8},{8,9},{9,10},{10,1... | collective-permute-start | bytes 92168 | tf_op jit(solution)/shard_map/ppermute | solution.py:20
  571.8 7.7 collective-permute-start.59
  594.3 7.6 collective-permute-start.63
  603.9 6.8 collective-permute-start.65
  613.9 7.6 collective-permute-start.67
  634.9 7.6 collective-permute-start.71
  654.2 7.6 collective-permute-start.75
  673.4 7.6 collective-permute-start.79
  692.6 7.6 collective-permute-start.83
  712.1 7.6 collective-permute-start.87
  733.9 7.7 collective-permute-start.91
  769.1 7.9 %collective-permute-start.95 = (f32[3,10,1,256]{3,2,1,0:T(1,128)S(1)}, f32[3,10,1,256]{3,2,1,0:T(1,128)S(1)}, u32[]{:S(2)}, u32[]{:S(2)}) collective-permute-start(f32[3,10,1,256]{3,2,1,0:T(1,128)S(1)} %get-tuple-element.70), channel_id=1, source_target_pairs={{0,1},{1,2},{2,3},{3,4},{4,5},{5,6},{6,7},{7,8},{8,9},{9,10},{10,1... | collective-permute-start | bytes 92168 | tf_op jit(solution)/shard_map/ppermute | solution.py:20
  (160 other events, 3500.4 us)
where the time goes:
time: 789 us; the launch traced here: 779 us
  starting transfers between devices  258 us (33%)
  local copies, waits for them, and re-layouts  245 us (31%)
  waiting for transfers between devices  164 us (21%)
  other arithmetic  108 us (14%)
    ppermute x48, waiting for transfers between devices, padded_2(): lax.ppermute(lax.slice_in_dim(block, block.shape[dim] - width, None, axis...  161 us
    ppermute x48, starting transfers between devices, padded_2(): lax.ppermute(lax.slice_in_dim(block, block.shape[dim] - width, None, axis...  146 us
    ppermute x48, starting transfers between devices, padded_2(): lax.ppermute(lax.slice_in_dim(block, 0, width, axis=dim), axis, backward)  113 us
    another operation x25, local copies, waits for them, and re-layouts, outgoing_weights(): jnp.stack([unity, bernoulli(difference), bernoulli(-difference)])  103 us
    reshape x2, local copies, waits for them, and re-layouts, coarsen_level(): reaction.reshape(3, 3, span_x // 2, 2, span_y // 2, 2, span_z // 2, 2)  45.4 us
    reshape x4, local copies, waits for them, and re-layouts, restrict_field(): field.reshape(3, span_x // 2, 2, span_y // 2, 2, span_z // 2, 2)  33.1 us
    squeeze x12, local copies, waits for them, and re-layouts, coarsen_level(): blocks[direction]  23 us
    reshape x4, local copies, waits for them, and re-layouts, prolong_field(): return spread.reshape(3, 2 * span_x, 2 * span_y, 2 * span_z)  22.7 us
  transfers between devices with their start and end apart: 96, of which 45 were waited for; matrix products, arithmetic and copies ran while one was open for 18% of the time, Pallas kernels for 0%

commit v1 on v0

v1 whole, which is shorter than its diff:
```python
import functools

import jax
import jax.numpy as jnp
from jax import lax
from jax.experimental import pallas as pl
from jax.experimental.pallas import tpu as pltpu
from jax.sharding import PartitionSpec as P

MESH = pl.DeviceIdType.MESH
LEVELS = 4
COARSE_SWEEPS = 6
REGIONS = 4
OMEGA = 0.8
STRENGTH = 8.0
ROWS = 8
NX = (8, 4, 2, 1)


def each(count, body):
    if count == 1:
        body(0)
        return

    def step(i, carry):
        body(i)
        return carry

    lax.fori_loop(0, count, step, 0)


def face_weights(difference):
    size = jnp.abs(difference)
    small = size < 0.5
    series = 1.0 / 362880.0
    for k in (40320.0, 5040.0, 720.0, 120.0, 24.0, 6.0, 2.0, 1.0):
        series = series * size + 1.0 / k
    below = jnp.where(small, series, jnp.exp(size) - 1.0)
    low = jnp.where(small, 1.0, size) / below
    low = jnp.where(size < 1e-4, 1.0 - 0.5 * size, low)
    high = low + size
    positive = difference > 0.0
    return jnp.where(positive, low, high), jnp.where(positive, high, low)


def kernel(counts, grad_in, pot_in, coup_in, region_in, contact_in, rates_in, out, *scratch):
    grad, pot, coup, region, contact, rates, in_sem = scratch[-7:]
    scratch = scratch[:-7]
    loads = {}
    for i, (name, source, target) in enumerate(
        (
            ("pot", pot_in, pot.at[pl.ds(1, 8)]),
            ("rates", rates_in, rates),
            ("region", region_in, region),
            ("contact", contact_in, contact),
            ("coup", coup_in, coup),
            ("grad", grad_in, grad),
        )
    ):
        loads[name] = pltpu.make_async_copy(source, target, in_sem.at[i])
        loads[name].start()
    weights, reaction, diag, inverse = (scratch[4 * i : 4 * i + 4] for i in range(4))
    sources = (None,) + tuple(scratch[16:19])
    fields = scratch[19:23]
    rows_halo, pot_y, send_y, send_x, recv_x, send_sem, recv_sem = scratch[23:]
    n_x, n_y = counts
    lanes = out.shape[-1]
    gx, gy = lax.axis_index("gx"), lax.axis_index("gy")
    x_low, x_high = lax.rem(gx + n_x - 1, n_x), lax.rem(gx + 1, n_x)
    y_low, y_high = lax.rem(gy + n_y - 1, n_y), lax.rem(gy + 1, n_y)
    beside = ((x_high, gy), (x_low, gy), (gx, y_high), (gx, y_low))

    barrier = pltpu.get_barrier_semaphore()
    for device in beside:
        pl.semaphore_signal(barrier, inc=1, device_id=device, device_id_type=MESH)
    pl.semaphore_wait(barrier, 4)

    tile = (ROWS, lanes)
    row_at = lax.broadcasted_iota(jnp.int32, tile, 0)
    lane_at = lax.broadcasted_iota(jnp.int32, tile, 1)
    wide = lambda row: jnp.broadcast_to(row, tile)
    down = lambda v, by: pltpu.roll(v, by % ROWS, 0) if by % ROWS else v
    along = lambda v, by: pltpu.roll(v, by % lanes, 1)

    done = [0]

    def exchange(parts):
        slot = done[0] % 2
        done[0] += 1
        copies = []
        for i, (source, target) in enumerate(parts):
            copy = pltpu.make_async_remote_copy(
                src_ref=source,
                dst_ref=target,
                send_sem=send_sem.at[i],
                recv_sem=recv_sem.at[slot, i],
                device_id=beside[i],
                device_id_type=MESH,
            )
            copy.start()
            copies.append(copy)
        for copy in copies:
            copy.wait()

    loads["pot"].wait()
    for side, at in ((0, ROWS - 1), (1, 0)):
        packed = wide(pot[1, at : at + 1, :])
        for x in range(1, 8):
            packed = jnp.where(row_at == x, wide(pot[x + 1, at : at + 1, :]), packed)
        send_y[side, 0] = packed
    exchange(
        [
            (pot.at[8], pot.at[0]),
            (pot.at[1], pot.at[9]),
            (send_y.at[0, 0], pot_y.at[0]),
            (send_y.at[1, 0], pot_y.at[1]),
        ]
    )
    is_low_x, is_high_x = gx == 0, gx == n_x - 1
    is_low_y, is_high_y = gy == 0, gy == n_y - 1
    pot[0] = jnp.where(is_low_x, 0.0, pot[0])
    pot[9] = jnp.where(is_high_x, 0.0, pot[9])
    pot_y[0] = jnp.where(is_low_y, 0.0, pot_y[0])
    pot_y[1] = jnp.where(is_high_y, 0.0, pot_y[1])

    for name in ("rates", "region", "contact", "coup"):
        loads[name].wait()

    def set_up(x):
        here = pot[x + 1]
        near = (
            pot[x + 2],
            pot[x],
            jnp.where(row_at == ROWS - 1, wide(pot_y[1, pl.ds(x, 1), :]), down(here, -1)),
            jnp.where(row_at == 0, wide(pot_y[0, pl.ds(x, 1), :]), down(here, 1)),
            jnp.where(lane_at == lanes - 1, 0.0, along(here, -1)),
            jnp.where(lane_at == 0, 0.0, along(here, 1)),
        )
        for k in range(6):
            plus, minus = face_weights(here - near[k])
            weights[0][x, 3 * k] = jnp.ones(tile, jnp.float32)
            weights[0][x, 3 * k + 1] = plus
            weights[0][x, 3 * k + 2] = minus
        at_contact = STRENGTH * contact[x].astype(jnp.float32)
        regions = region[x]
        for c in range(3):
            extra = jnp.full(tile, rates[0, c])
            for pick in range(1, REGIONS):
                extra = jnp.where(regions == pick, rates[pick, c], extra)
            for d in range(3):
                value = coup[c, d, x]
                reaction[0][x, 3 * c + d] = value + (extra + at_contact) if c == d else value

    each(NX[0], set_up)

    def finish_level(level):
        w, r, span = weights[level], reaction[level], 1 << level

        def body(x):
            m = [[r[x, 3 * col + row] for col in range(3)] for row in range(3)]
            for c in range(3):
                total = w[x, c]
                for k in range(1, 6):
                    total = total + w[x, 3 * k + c]
                m[c][c] = m[c][c] + total
                diag[level][x, c] = m[c][c]

            def cofactor(i, j):
                i1, i2, j1, j2 = (i + 1) % 3, (i + 2) % 3, (j + 1) % 3, (j + 2) % 3
                return m[i1][j1] * m[i2][j2] - m[i1][j2] * m[i2][j1]

            cof = [[cofactor(i, j) for j in range(3)] for i in range(3)]
            det = m[0][0] * cof[0][0] + m[0][1] * cof[0][1] + m[0][2] * cof[0][2]
            scale = OMEGA / det
            for i in range(3):
                for j in range(3):
                    inverse[level][x, 3 * i + j] = cof[j][i] * scale

        each(NX[level], body)

    def mask_level(level):
        w, span, last = weights[level], 1 << level, NX[level] - 1
        for c in range(3):
            w[last, c] = jnp.where(is_high_x, 0.0, w[last, c])
            w[0, 3 + c] = jnp.where(is_low_x, 0.0, w[0, 3 + c])
        off_high = jnp.logical_and(row_at >= ROWS - span, is_high_y)
        off_low = jnp.logical_and(row_at < span, is_low_y)
        off_up, off_down = lane_at >= lanes - span, lane_at < span

        def body(x):
            for k, off in ((2, off_high), (3, off_low), (4, off_up), (5, off_down)):
                for c in range(3):
                    w[x, 3 * k + c] = jnp.where(off, 0.0, w[x, 3 * k + c])

        each(NX[level], body)

    def pair_tools(level):
        span = 1 << level
        odd_row = (row_at & span) != 0
        odd_lane = (lane_at & span) != 0

        def high_row(v):
            return jnp.where(odd_row, v, down(v, -span))

        def low_row(v):
            return jnp.where(odd_row, down(v, span), v)

        def high_lane(v):
            return jnp.where(odd_lane, v, along(v, -span))

        def low_lane(v):
            return jnp.where(odd_lane, along(v, span), v)

        def rows(v):
            return v + jnp.where(odd_row, down(v, span), down(v, -span))

        def lanes_(v):
            return v + jnp.where(odd_lane, along(v, span), along(v, -span))

        return high_row, low_row, high_lane, low_lane, rows, lanes_

    def coarsen(level):
        high_row, low_row, high_lane, low_lane, rows, lanes_ = pair_tools(level)
        w, r, w_next, r_next = weights[level], reaction[level], weights[level + 1], reaction[level + 1]

        def body(x):
            for c in range(3):
                w_next[x, c] = lanes_(rows(w[2 * x + 1, c]))
                w_next[x, 3 + c] = lanes_(rows(w[2 * x, 3 + c]))
                pair = lambda k: w[2 * x, 3 * k + c] + w[2 * x + 1, 3 * k + c]
                w_next[x, 6 + c] = lanes_(high_row(pair(2)))
                w_next[x, 9 + c] = lanes_(low_row(pair(3)))
                w_next[x, 12 + c] = high_lane(rows(pair(4)))
                w_next[x, 15 + c] = low_lane(rows(pair(5)))
            for i in range(9):
                r_next[x, i] = lanes_(rows(r[2 * x, i] + r[2 * x + 1, i]))

        each(NX[level + 1], body)

    for level in range(LEVELS):
        finish_level(level)
        if level < LEVELS - 1:
            coarsen(level)
        mask_level(level)

    def source(level, x):
        if level == 0:
            return [grad[c, x] for c in range(3)]
        return [sources[level][x, c] for c in range(3)]

    def solve(level, x, r):
        v = inverse[level]
        return [v[x, 3 * c] * r[0] + v[x, 3 * c + 1] * r[1] + v[x, 3 * c + 2] * r[2] for c in range(3)]

    def share(level, at):
        slot, f, count = done[0] % 2, fields[level], NX[level]
        if level < 2:
            for side, row in ((0, ROWS - 1), (1, 0)):
                for c in range(3):
                    packed = wide(f[at, 1, c, row : row + 1, :])
                    for x in range(1, count):
                        packed = jnp.where(row_at == x, wide(f[at, x + 1, c, row : row + 1, :]), packed)
                    send_y[side, c] = packed
            exchange(
                [
                    (f.at[at, count], f.at[at, 0]),
                    (f.at[at, 1], f.at[at, count + 1]),
                    (send_y.at[0], rows_halo.at[slot, 0]),
                    (send_y.at[1], rows_halo.at[slot, 1]),
                ]
            )
            return slot
        for side, row in ((0, ROWS - 1), (1, 0)):
            packed = wide(f[at, 1, 0, row : row + 1, :])
            for x in range(count):
                for c in range(3):
                    packed = jnp.where(row_at == 4 * x + c, wide(f[at, x + 1, c, row : row + 1, :]), packed)
            send_y[side, 0] = packed
        for side, x in ((0, count), (1, 1)):
            by_four = row_at & 3
            packed = jnp.where(by_four == 0, f[at, x, 0], jnp.where(by_four == 1, f[at, x, 1], f[at, x, 2]))
            send_x[side] = packed
        exchange(
            [
                (send_x.at[0], recv_x.at[slot, 0]),
                (send_x.at[1], recv_x.at[slot, 1]),
                (send_y.at[0, 0], rows_halo.at[slot, 0, 0]),
                (send_y.at[1, 0], rows_halo.at[slot, 1, 0]),
            ]
        )
        for side, x in ((0, 0), (1, count + 1)):
            for c in range(3):
                value = wide(recv_x[slot, side, c : c + 1, :])
                if level == 2:
                    value = jnp.where(row_at < 4, value, wide(recv_x[slot, side, 4 + c : 5 + c, :]))
                f[at, x, c] = value
        return slot

    def residual(level, at, slot, x):
        f, w, r, span = fields[level], weights[level], reaction[level], 1 << level
        u = [f[at, x + 1, c] for c in range(3)]
        b = source(level, x)
        left = []
        for c in range(3):
            if level < 2:
                row_high, row_low = (rows_halo[slot, side, c, pl.ds(x, 1), :] for side in (1, 0))
            else:
                row_high, row_low = (rows_halo[slot, side, 0, pl.ds(4 * x + c, 1), :] for side in (1, 0))
            near = (
                f[at, x + 2, c],
                f[at, x, c],
                jnp.where(row_at >= ROWS - span, wide(row_high), down(u[c], -span)),
                jnp.where(row_at < span, wide(row_low), down(u[c], span)),
                along(u[c], -span),
                along(u[c], span),
            )
            value = b[c] - diag[level][x, c] * u[c]
            for k in range(6):
                value = value + w[x, 3 * k + c] * near[k]
            for d in range(3):
                if d != c:
                    value = value - r[x, 3 * d + c] * u[d]
            left.append(value)
        return u, left

    def sweep(level, at, slot, last=False):
        def body(x):
            u, left = residual(level, at, slot, x)
            step = solve(level, x, left)
            for c in range(3):
                if last:
                    out[c, x] = u[c] + step[c]
                else:
                    fields[level][1 - at, x + 1, c] = u[c] + step[c]

        each(NX[level], body)
        return 1 - at

    def restrict(level, at, slot):
        rows, lanes_ = pair_tools(level)[4:]

        def body(x):
            left = [residual(level, at, slot, 2 * x + i)[1] for i in range(2)]
            total = [lanes_(rows(left[0][c] + left[1][c])) for c in range(3)]
            first = solve(level + 1, x, total)
            for c in range(3):
                sources[level + 1][x, c] = total[c]
                fields[level + 1][0, x + 1, c] = first[c]

        each(NX[level + 1], body)

    def cycle(level, at, last=False):
        if level == LEVELS - 1:
            for _ in range(COARSE_SWEEPS - 1):
                at = sweep(level, at, share(level, at))
            return at
        restrict(level, at, share(level, at))
        e = cycle(level + 1, 0)

        def add(x):
            for c in range(3):
                for i in range(2):
                    fields[level][at, 2 * x + 1 + i, c] += fields[level + 1][e, x + 1, c]

        each(NX[level + 1], add)
        return sweep(level, at, share(level, at), last)

    def start(x):
        for c, value in enumerate(solve(0, x, source(0, x))):
            fields[0][0, x + 1, c] = value

    loads["grad"].wait()
    each(NX[0], start)
    at = cycle(0, 0)
    at = sweep(0, at, share(0, at))
    cycle(0, at, last=True)


def local(counts, gradient, potential, coupling, region, contact, rates):
    nz = potential.shape[-1]
    tile = (ROWS, nz)
    f32 = jnp.float32
    scratch = []
    for parts in (18, 9, 3, 9):
        scratch += [pltpu.VMEM((n, parts) + tile, f32) for n in NX]
    scratch += [pltpu.VMEM((n, 3) + tile, f32) for n in NX[1:]]
    scratch += [pltpu.VMEM((2, n + 2, 3) + tile, f32) for n in NX]
    scratch += [
        pltpu.VMEM((2, 2, 3) + tile, f32),
        pltpu.VMEM((2,) + tile, f32),
        pltpu.VMEM((2, 3) + tile, f32),
        pltpu.VMEM((2,) + tile, f32),
        pltpu.VMEM((2, 2) + tile, f32),
        pltpu.SemaphoreType.DMA((4,)),
        pltpu.SemaphoreType.DMA((2, 4)),
        pltpu.VMEM(gradient.shape, f32),
        pltpu.VMEM((10,) + tile, f32),
        pltpu.VMEM(coupling.shape, f32),
        pltpu.VMEM(region.shape, jnp.int32),
        pltpu.VMEM(contact.shape, jnp.int32),
        pltpu.SMEM(rates.shape, f32),
        pltpu.SemaphoreType.DMA((6,)),
    ]
    vmem = pl.BlockSpec(memory_space=pltpu.VMEM)
    return pl.pallas_call(
        functools.partial(kernel, counts),
        out_shape=jax.ShapeDtypeStruct(gradient.shape, f32),
        in_specs=[pl.BlockSpec(memory_space=pltpu.HBM)] * 6,
        out_specs=vmem,
        scratch_shapes=scratch,
        compiler_params=pltpu.CompilerParams(
            collective_id=0, has_side_effects=True, vmem_limit_bytes=40 * 1024 * 1024
        ),
    )(gradient, potential, coupling, region, contact, rates)


def solution(mesh):
    placed = (
        P(None, "gx", "gy", None),
        P("gx", "gy", None),
        P(None, None, "gx", "gy", None),
        P("gx", "gy", None),
        P("gx", "gy", None),
        P(),
    )
    counts = (mesh.shape["gx"], mesh.shape["gy"])
    return jax.shard_map(
        functools.partial(local, counts),
        mesh=mesh,
        in_specs=placed,
        out_specs=P(None, "gx", "gy", None),
        check_vma=False,
    )
```

time: 789 us -> 127 us (0.16)
  the two profiles are of different devices: /device:TPU:134 before, /device:TPU:1 now
where the time goes in v1:
time: 127 us
  Pallas kernels  121 us (95%)
  local copies, waits for them, and re-layouts  5.87 us (5%)
    pallas_call x1, Pallas kernels, local(): pl.pallas_call(functools.partial(kernel, counts), out_shape=jax.ShapeDtyp...  121 us
    unnamed x13, local copies, waits for them, and re-layouts  5.87 us

profile of v1, /device:TPU:1, one launch (start us, length us, event | category | flops | bytes accessed | tf_op | source)
XLA Modules:
  0.0 127.1 jit_solution(8049180414289237280)
XLA Ops:
  0.0 0.0 copy-start
  0.0 1.1 copy-done
  1.1 0.0 copy-start.1
  1.1 0.9 copy-done.1
  2.0 0.0 copy-start.2
  2.0 0.8 copy-done.2
  2.8 0.0 copy-start.3
  2.8 0.8 copy-done.3
  3.7 0.0 copy-start.4
  3.7 0.8 copy-done.4
  4.5 0.0 copy-start.5
  4.5 0.7 copy-done.5
  5.2 121.2 %shard_map.64 = f32[3,8,8,256]{3,2,1,0:T(8,128)S(1)} custom-call(f32[3,8,8,256]{3,2,1,0:T(8,128)S(1)} %copy-done.1, f32[8,8,256]{2,1,0:T(8,128)S(1)} %copy-done.2, f32[3,3,8,8,256]{4,3,2,1,0:T(8,128)S(1)} %copy-done, s32[8,8,256]{2,1,0:T(8,128)S(1)} %copy-done.3, s32[8,8,256]{2,1,0:T(8,128)S(1)} %copy-done.4, f32[4,3]{1,0:T(4,128)S(1)} %copy-done.5), custom_call_target="tpu_custom_call" | custom-call | tf_op jit(solution)/shard_map/pallas_call | solution.py:405
  126.4 0.7 copy.8
Async XLA Ops:
  0.0 1.1 copy-start
  1.1 0.9 copy-start.1
  2.0 0.8 copy-start.2
  2.8 0.8 copy-start.3
  3.7 0.8 copy-start.4
  4.5 0.7 copy-start.5

commit v2 on v1

--- a/solution.py
+++ b/solution.py
@@ -15,6 +15,14 @@
 STRENGTH = 8.0
 ROWS = 8
 NX = (8, 4, 2, 1)
+RADIUS = 3
+WINDOW = [
+    (i, j)
+    for i in range(-RADIUS, RADIUS + 1)
+    for j in range(-RADIUS, RADIUS + 1)
+    if 0 < abs(i) + abs(j) <= RADIUS
+]
+SLOTS = 8
 
 
 def each(count, body):
@@ -26,7 +34,7 @@
         body(i)
         return carry
 
-    lax.fori_loop(0, count, step, 0)
+    lax.fori_loop(0, count, step, 0, unroll=count)
 
 
 def face_weights(difference):
@@ -62,7 +70,9 @@
     weights, reaction, diag, inverse = (scratch[4 * i : 4 * i + 4] for i in range(4))
     sources = (None,) + tuple(scratch[16:19])
     fields = scratch[19:23]
-    rows_halo, pot_y, send_y, send_x, recv_x, send_sem, recv_sem = scratch[23:]
+    rows_halo, pot_y, send_y, send_x, recv_x, send_sem, recv_sem = scratch[23:30]
+    w_own, r_own, coef_send, coef_recv, cell_send, cell_recv, e_rows = scratch[30:37]
+    coef_send_sem, coef_recv_sem, cell_send_sem, cell_recv_sem = scratch[37:]
     n_x, n_y = counts
     lanes = out.shape[-1]
     gx, gy = lax.axis_index("gx"), lax.axis_index("gy")
@@ -71,9 +81,10 @@
     beside = ((x_high, gy), (x_low, gy), (gx, y_high), (gx, y_low))
 
     barrier = pltpu.get_barrier_semaphore()
-    for device in beside:
+    around = [(lax.rem(gx + n_x + i, n_x), lax.rem(gy + n_y + j, n_y)) for i, j in WINDOW]
+    for device in around:
         pl.semaphore_signal(barrier, inc=1, device_id=device, device_id_type=MESH)
-    pl.semaphore_wait(barrier, 4)
+    pl.semaphore_wait(barrier, len(WINDOW))
 
     tile = (ROWS, lanes)
     row_at = lax.broadcasted_iota(jnp.int32, tile, 0)
@@ -88,7 +99,8 @@
         slot = done[0] % 2
         done[0] += 1
         copies = []
-        for i, (source, target) in enumerate(parts):
+        for i in (2, 3, 0, 1):
+            source, target = parts[i]
             copy = pltpu.make_async_remote_copy(
                 src_ref=source,
                 dst_ref=target,
@@ -99,8 +111,32 @@
             )
             copy.start()
             copies.append(copy)
-        for copy in copies:
-            copy.wait()
+
+        def wait():
+            for copy in copies:
+                copy.wait()
+
+        return wait
+
+    def gather(source, target, send, recv):
+        copies = []
+        for n, device in enumerate(around):
+            copy = pltpu.make_async_remote_copy(
+                src_ref=source,
+                dst_ref=target.at[n],
+                send_sem=send.at[n],
+                recv_sem=recv.at[n],
+                device_id=device,
+                device_id_type=MESH,
+            )
+            copy.start()
+            copies.append(copy)
+
+        def wait():
+            for copy in copies:
+                copy.wait()
+
+        return wait
 
     loads["pot"].wait()
     for side, at in ((0, ROWS - 1), (1, 0)):
@@ -108,7 +144,7 @@
         for x in range(1, 8):
             packed = jnp.where(row_at == x, wide(pot[x + 1, at : at + 1, :]), packed)
         send_y[side, 0] = packed
-    exchange(
+    wait = exchange(
         [
             (pot.at[8], pot.at[0]),
             (pot.at[1], pot.at[9]),
@@ -116,31 +152,24 @@
             (send_y.at[1, 0], pot_y.at[1]),
         ]
     )
-    is_low_x, is_high_x = gx == 0, gx == n_x - 1
-    is_low_y, is_high_y = gy == 0, gy == n_y - 1
-    pot[0] = jnp.where(is_low_x, 0.0, pot[0])
-    pot[9] = jnp.where(is_high_x, 0.0, pot[9])
-    pot_y[0] = jnp.where(is_low_y, 0.0, pot_y[0])
-    pot_y[1] = jnp.where(is_high_y, 0.0, pot_y[1])
-
     for name in ("rates", "region", "contact", "coup"):
         loads[name].wait()
+
+    def put_faces(x, first, near):
+        here = pot[x + 1]
+        for k, value in enumerate(near):
+            plus, minus = face_weights(here - value)
+            weights[0][x, 3 * (first + k)] = jnp.ones(tile, jnp.float32)
+            weights[0][x, 3 * (first + k) + 1] = plus
+            weights[0][x, 3 * (first + k) + 2] = minus
 
     def set_up(x):
         here = pot[x + 1]
         near = (
-            pot[x + 2],
-            pot[x],
-            jnp.where(row_at == ROWS - 1, wide(pot_y[1, pl.ds(x, 1), :]), down(here, -1)),
-            jnp.where(row_at == 0, wide(pot_y[0, pl.ds(x, 1), :]), down(here, 1)),
             jnp.where(lane_at == lanes - 1, 0.0, along(here, -1)),
             jnp.where(lane_at == 0, 0.0, along(here, 1)),
         )
-        for k in range(6):
-            plus, minus = face_weights(here - near[k])
-            weights[0][x, 3 * k] = jnp.ones(tile, jnp.float32)
-            weights[0][x, 3 * k + 1] = plus
-            weights[0][x, 3 * k + 2] = minus
+        put_faces(x, 4, near)
         at_contact = STRENGTH * contact[x].astype(jnp.float32)
         regions = region[x]
         for c in range(3):
@@ -152,6 +181,25 @@
                 reaction[0][x, 3 * c + d] = value + (extra + at_contact) if c == d else value
 
     each(NX[0], set_up)
+    wait()
+    is_low_x, is_high_x = gx == 0, gx == n_x - 1
+    is_low_y, is_high_y = gy == 0, gy == n_y - 1
+    pot[0] = jnp.where(is_low_x, 0.0, pot[0])
+    pot[9] = jnp.where(is_high_x, 0.0, pot[9])
+    pot_y[0] = jnp.where(is_low_y, 0.0, pot_y[0])
+    pot_y[1] = jnp.where(is_high_y, 0.0, pot_y[1])
+
+    def cross_faces(x):
+        here = pot[x + 1]
+        near = (
+            pot[x + 2],
+            pot[x],
+            jnp.where(row_at == ROWS - 1, wide(pot_y[1, pl.ds(x, 1), :]), down(here, -1)),
+            jnp.where(row_at == 0, wide(pot_y[0, pl.ds(x, 1), :]), down(here, 1)),
+        )
+        put_faces(x, 0, near)
+
+    each(NX[0], cross_faces)
 
     def finish_level(level):
         w, r, span = weights[level], reaction[level], 1 << level
@@ -221,7 +269,8 @@
 
     def coarsen(level):
         high_row, low_row, high_lane, low_lane, rows, lanes_ = pair_tools(level)
-        w, r, w_next, r_next = weights[level], reaction[level], weights[level + 1], reaction[level + 1]
+        w, r = weights[level], reaction[level]
+        w_next, r_next = (w_own, r_own) if level == LEVELS - 2 else (weights[level + 1], reaction[level + 1])
 
         def body(x):
             for c in range(3):
@@ -237,11 +286,105 @@
 
         each(NX[level + 1], body)
 
-    for level in range(LEVELS):
-        finish_level(level)
-        if level < LEVELS - 1:
-            coarsen(level)
-        mask_level(level)
+    slot_at = lane_at & (SLOTS - 1)
+    cells = [(-i, -j) for i, j in WINDOW] + [(0, 0)]
+
+    def columns(row_of):
+        for t in range(2 * RADIUS + 1):
+            packed = jnp.zeros(tile, jnp.float32)
+            for n, (i, j) in enumerate(cells):
+                if j + RADIUS == t:
+                    packed = jnp.where(row_at == i + RADIUS, wide(row_of(n)), packed)
+            yield t, packed
+
+    def send_coefficients():
+        fields_ = [w_own[0, i] for i in range(18)] + [r_own[0, i] for i in range(9)]
+        for row in range(4):
+            part = fields_[SLOTS * row : SLOTS * row + SLOTS]
+            packed = part[0]
+            for i in range(1, len(part)):
+                packed = jnp.where(slot_at == i, part[i], packed)
+            coef_send[row : row + 1, :] = packed[0:1, :]
+        return gather(coef_send, coef_recv, coef_send_sem, coef_recv_sem)
+
+    def take_coefficients():
+        top = LEVELS - 1
+        w, r = weights[top], reaction[top]
+        for row in range(4):
+            row_of = lambda n: coef_recv[n, row : row + 1, :] if n < len(WINDOW) else coef_send[row : row + 1, :]
+            count = min(SLOTS, 27 - SLOTS * row)
+            made = [jnp.full(tile, 1.0 if SLOTS * row + i in (18, 22, 26) else 0.0) for i in range(count)]
+            for t, packed in columns(row_of):
+                for i in range(count):
+                    made[i] = jnp.where(slot_at == t, along(packed, t - i), made[i])
+            for i in range(count):
+                at = SLOTS * row + i
+                if at < 18:
+                    w[0, at] = made[i]
+                else:
+                    r[0, at - 18] = made[i]
+        finish_level(top)
+        x_at, y_at = row_at + (gx - RADIUS), slot_at + (gy - RADIUS)
+        offs = (
+            jnp.logical_or(x_at == n_x - 1, x_at == -1),
+            jnp.logical_or(x_at == 0, x_at == n_x),
+            jnp.logical_or(y_at == n_y - 1, y_at == -1),
+            jnp.logical_or(y_at == 0, y_at == n_y),
+            lane_at >= lanes - SLOTS,
+            lane_at < SLOTS,
+        )
+        for k, off in enumerate(offs):
+            for c in range(3):
+                w[0, 3 * k + c] = jnp.where(off, 0.0, w[0, 3 * k + c])
+
+    def share_cells(which, values):
+        packed = jnp.where(slot_at == 0, values[0], jnp.where(slot_at == 1, values[1], values[2]))
+        cell_send[which] = packed[0:1, :]
+        gather(cell_send.at[which], cell_recv.at[which], cell_send_sem, cell_recv_sem.at[which])()
+        made = [jnp.zeros(tile, jnp.float32) for _ in range(3)]
+        row_of = lambda n: cell_recv[which, n] if n < len(WINDOW) else cell_send[which]
+        for t, packed in columns(row_of):
+            for c in range(3):
+                made[c] = jnp.where(slot_at == t, along(packed, t - c), made[c])
+        return made
+
+    def spread(value, t):
+        value = jnp.where(slot_at == t, value, 0.0)
+        for bit in (1, 2, 4):
+            value = value + along(value, -bit if t & bit else bit)
+        return value
+
+    def window_sweep(b, u):
+        top = LEVELS - 1
+        w, r = weights[top], reaction[top]
+        left = []
+        for c in range(3):
+            value = b[c] - diag[top][0, c] * u[c]
+            near = (down(u[c], -1), down(u[c], 1), along(u[c], -1), along(u[c], 1), along(u[c], -SLOTS), along(u[c], SLOTS))
+            for k in range(6):
+                value = value + w[0, 3 * k + c] * near[k]
+            for d in range(3):
+                if d != c:
+                    value = value - r[0, 3 * d + c] * u[d]
+            left.append(value)
+        step = solve(top, 0, left)
+        return [u[c] + step[c] for c in range(3)]
+
+    def coarsest(own):
+        b = share_cells(0, own)
+        u = solve(LEVELS - 1, 0, b)
+        for _ in range(RADIUS):
+            u = window_sweep(b, u)
+        u = [spread(value, RADIUS) for value in u]
+        u = share_cells(1, [value[RADIUS : RADIUS + 1, :] for value in u])
+        for _ in range(COARSE_SWEEPS - 1 - RADIUS):
+            u = window_sweep(b, u)
+        for c in range(3):
+            for j in range(3):
+                e_rows[c, j] = spread(u[c], RADIUS - 1 + j)
+
+    def e_at(c, i, j):
+        return wide(e_rows[c, 1 + j, RADIUS + i : RADIUS + i + 1, :])
 
     def source(level, x):
         if level == 0:
@@ -252,7 +395,7 @@
         v = inverse[level]
         return [v[x, 3 * c] * r[0] + v[x, 3 * c + 1] * r[1] + v[x, 3 * c + 2] * r[2] for c in range(3)]
 
-    def share(level, at):
+    def share(level, at, beside_it=lambda: None):
         slot, f, count = done[0] % 2, fields[level], NX[level]
         if level < 2:
             for side, row in ((0, ROWS - 1), (1, 0)):
@@ -261,7 +404,7 @@
                     for x in range(1, count):
                         packed = jnp.where(row_at == x, wide(f[at, x + 1, c, row : row + 1, :]), packed)
                     send_y[side, c] = packed
-            exchange(
+            wait = exchange(
                 [
                     (f.at[at, count], f.at[at, 0]),
                     (f.at[at, 1], f.at[at, count + 1]),
@@ -269,6 +412,8 @@
                     (send_y.at[1], rows_halo.at[slot, 1]),
                 ]
             )
+            beside_it()
+            wait()
             return slot
         for side, row in ((0, ROWS - 1), (1, 0)):
             packed = wide(f[at, 1, 0, row : row + 1, :])
@@ -280,7 +425,7 @@
             by_four = row_at & 3
             packed = jnp.where(by_four == 0, f[at, x, 0], jnp.where(by_four == 1, f[at, x, 1], f[at, x, 2]))
             send_x[side] = packed
-        exchange(
+        wait = exchange(
             [
                 (send_x.at[0], recv_x.at[slot, 0]),
                 (send_x.at[1], recv_x.at[slot, 1]),
@@ -288,6 +433,8 @@
                 (send_y.at[1, 0], rows_halo.at[slot, 1, 0]),
             ]
         )
+        beside_it()
+        wait()
         for side, x in ((0, 0), (1, count + 1)):
             for c in range(3):
                 value = wide(recv_x[slot, side, c : c + 1, :])
@@ -342,6 +489,9 @@
         def body(x):
             left = [residual(level, at, slot, 2 * x + i)[1] for i in range(2)]
             total = [lanes_(rows(left[0][c] + left[1][c])) for c in range(3)]
+            if level == LEVELS - 2:
+                coarsest(total)
+                return
             first = solve(level + 1, x, total)
             for c in range(3):
                 sources[level + 1][x, c] = total[c]
@@ -349,18 +499,28 @@
 
         each(NX[level + 1], body)
 
-    def cycle(level, at, last=False):
-        if level == LEVELS - 1:
-            for _ in range(COARSE_SWEEPS - 1):
-                at = sweep(level, at, share(level, at))
-            return at
-        restrict(level, at, share(level, at))
-        e = cycle(level + 1, 0)
+    def cycle(level, at, besides, last=False):
+        f = fields[level]
+        slot = share(level, at, besides[level])
+        restrict(level, at, slot)
+        if level == LEVELS - 2:
+            for c in range(3):
+                own = e_at(c, 0, 0)
+                f[at, 0, c] += e_at(c, -1, 0)
+                f[at, 1, c] += own
+                f[at, 2, c] += own
+                f[at, 3, c] += e_at(c, 1, 0)
+            for side in range(2):
+                step = [e_at(c, 0, 2 * side - 1) for c in range(3)]
+                by_four = row_at & 3
+                rows_halo[slot, side, 0] += jnp.where(by_four == 0, step[0], jnp.where(by_four == 1, step[1], step[2]))
+            return sweep(level, at, slot)
+        e = cycle(level + 1, 0, besides)
 
         def add(x):
             for c in range(3):
                 for i in range(2):
-                    fields[level][at, 2 * x + 1 + i, c] += fields[level + 1][e, x + 1, c]
+                    f[at, 2 * x + 1 + i, c] += fields[level + 1][e, x + 1, c]
 
         each(NX[level + 1], add)
         return sweep(level, at, share(level, at), last)
@@ -369,11 +529,30 @@
         for c, value in enumerate(solve(0, x, source(0, x))):
             fields[0][0, x + 1, c] = value
 
+    finish_level(0)
     loads["grad"].wait()
     each(NX[0], start)
-    at = cycle(0, 0)
+    pending = []
+
+    def make_levels():
+        coarsen(0)
+        mask_level(0)
+        finish_level(1)
+        coarsen(1)
+        mask_level(1)
+        finish_level(2)
+        coarsen(2)
+        mask_level(2)
+        pending.append(send_coefficients())
+
+    def take():
+        pending[0]()
+        take_coefficients()
+
+    nothing = lambda: None
+    at = cycle(0, 0, (make_levels, take, nothing))
     at = sweep(0, at, share(0, at))
-    cycle(0, at, last=True)
+    cycle(0, at, (nothing,) * 3, last=True)
 
 
 def local(counts, gradient, potential, coupling, region, contact, rates):
@@ -385,6 +564,7 @@
         scratch += [pltpu.VMEM((n, parts) + tile, f32) for n in NX]
     scratch += [pltpu.VMEM((n, 3) + tile, f32) for n in NX[1:]]
     scratch += [pltpu.VMEM((2, n + 2, 3) + tile, f32) for n in NX]
+    wide_window = len(WINDOW)
     scratch += [
         pltpu.VMEM((2, 2, 3) + tile, f32),
         pltpu.VMEM((2,) + tile, f32),
@@ -393,6 +573,17 @@
         pltpu.VMEM((2, 2) + tile, f32),
         pltpu.SemaphoreType.DMA((4,)),
         pltpu.SemaphoreType.DMA((2, 4)),
+        pltpu.VMEM((1, 18) + tile, f32),
+        pltpu.VMEM((1, 9) + tile, f32),
+        pltpu.VMEM((4, nz), f32),
+        pltpu.VMEM((wide_window, 4, nz), f32),
+        pltpu.VMEM((2, 1, nz), f32),
+        pltpu.VMEM((2, wide_window, 1, nz), f32),
+        pltpu.VMEM((3, 3) + tile, f32),
+        pltpu.SemaphoreType.DMA((wide_window,)),
+        pltpu.SemaphoreType.DMA((wide_window,)),
+        pltpu.SemaphoreType.DMA((wide_window,)),
+        pltpu.SemaphoreType.DMA((2, wide_window)),
         pltpu.VMEM(gradient.shape, f32),
         pltpu.VMEM((10,) + tile, f32),
         pltpu.VMEM(coupling.shape, f32),
@@ -409,7 +600,7 @@
         out_specs=vmem,
         scratch_shapes=scratch,
         compiler_params=pltpu.CompilerParams(
-            collective_id=0, has_side_effects=True, vmem_limit_bytes=40 * 1024 * 1024
+            collective_id=0, has_side_effects=True, vmem_limit_bytes=60 * 1024 * 1024
         ),
     )(gradient, potential, coupling, region, contact, rates)
 

time: 127 us -> 94.2 us (0.74)
  Pallas kernels: 121 us -> 92.5 us
  local copies, waits for them, and re-layouts: 5.87 us -> 1.62 us
    pallas_call x1, Pallas kernels: 121 us -> 92.5 us  [local(): pl.pallas_call(functools.partial(kernel, counts), out_shape=jax.ShapeDtyp...]
    unnamed x13 -> x1, local copies, waits for them, and re-layouts: 5.87 us -> 1.62 us
where the time goes in v2:
time: 94.2 us; the launch traced here: 94.1 us
  Pallas kernels  92.5 us (98%)
  local copies, waits for them, and re-layouts  1.62 us (2%)
    pallas_call x1, Pallas kernels, local(): pl.pallas_call(functools.partial(kernel, counts), out_shape=jax.ShapeDtyp...  92.5 us

profile of v2, /device:TPU:1, one launch (start us, length us, event | category | flops | bytes accessed | tf_op | source)
XLA Modules:
  0.0 94.1 jit_solution(16405223825032398883)
XLA Ops:
  0.0 92.5 %shard_map.64 = f32[3,8,8,256]{3,2,1,0:T(8,128)} custom-call(f32[3,8,8,256]{3,2,1,0:T(8,128)} %grad_in.1, f32[8,8,256]{2,1,0:T(8,128)} %pot_in.1, f32[3,3,8,8,256]{4,3,2,1,0:T(8,128)} %coup_in.1, s32[8,8,256]{2,1,0:T(8,128)} %region_in.1, s32[8,8,256]{2,1,0:T(8,128)} %contact_in.1, f32[4,3]{1,0:T(4,128)} %rates_in.1), custom_call_target="tpu_custom_call" | custom-call | tf_op jit(solution)/shard_map/pallas_call | solution.py:596
  92.5 1.6 %copy.8 = f32[3,8,8,256]{3,2,1,0:T(8,128)} copy(f32[3,8,8,256]{3,2,1,0:T(8,128)} %shard_map.64) | data formatting | bytes 393216

commit v3 on v2

--- a/solution.py
+++ b/solution.py
@@ -16,13 +16,22 @@
 ROWS = 8
 NX = (8, 4, 2, 1)
 RADIUS = 3
-WINDOW = [
-    (i, j)
-    for i in range(-RADIUS, RADIUS + 1)
-    for j in range(-RADIUS, RADIUS + 1)
-    if 0 < abs(i) + abs(j) <= RADIUS
-]
 SLOTS = 8
+
+
+def around(shape, far):
+    reach = range(-6, 7)
+    distance = lambda i, j: min(abs(i - a) + abs(j - b) for a, b in shape)
+    found = [(i, j) for i in reach for j in reach if distance(i, j) <= far and (i, j) != (0, 0)]
+    return sorted(found, key=lambda o: -abs(o[0]) - abs(o[1]))
+
+
+OWN = [(0, 0)]
+SQUARE = [(i, j) for i in (-1, 0, 1) for j in (-1, 0, 1)]
+INNER = around(OWN, 2)
+OUTER = [o for o in around(OWN, 3) if o not in INNER]
+FOURTH = around(SQUARE, 2)
+THIRD = around(SQUARE, 3)
 
 
 def each(count, body):
@@ -70,9 +79,13 @@
     weights, reaction, diag, inverse = (scratch[4 * i : 4 * i + 4] for i in range(4))
     sources = (None,) + tuple(scratch[16:19])
     fields = scratch[19:23]
-    rows_halo, pot_y, send_y, send_x, recv_x, send_sem, recv_sem = scratch[23:30]
-    w_own, r_own, coef_send, coef_recv, cell_send, cell_recv, e_rows = scratch[30:37]
-    coef_send_sem, coef_recv_sem, cell_send_sem, cell_recv_sem = scratch[37:]
+    rows_halo, pot_y, send_y, send_sem, recv_sem = scratch[23:28]
+    w_own, r_own, w_wide, r_wide, diag_wide, inverse_wide, u_wide, b_wide, e_rows = scratch[28:37]
+    mid_send, mid_recv, low_send, low_recv, mid_cell, mid_cells, low_cell, low_cells = scratch[37:45]
+    mid_send_sem, mid_recv_sem, low_send_sem, low_recv_sem, p_send, p_recv, q_send, q_recv = scratch[45:53]
+    ring_u, ring_b, ring_w, ring_r, ring_diag, ring_inverse, ring_out = scratch[53:60]
+    pair_own, pair_x, pair_y_send, pair_y, pair_corner_send, pair_corner, pair_send_sem, pair_recv_sem = scratch[60:68]
+    coef_own, coef_x, coef_y_send, coef_y, coef_send_sem, coef_recv_sem = scratch[68:]
     n_x, n_y = counts
     lanes = out.shape[-1]
     gx, gy = lax.axis_index("gx"), lax.axis_index("gy")
@@ -81,10 +94,11 @@
     beside = ((x_high, gy), (x_low, gy), (gx, y_high), (gx, y_low))
 
     barrier = pltpu.get_barrier_semaphore()
-    around = [(lax.rem(gx + n_x + i, n_x), lax.rem(gy + n_y + j, n_y)) for i, j in WINDOW]
-    for device in around:
+    at_offset = lambda i, j: (lax.rem(gx + n_x + i, n_x), lax.rem(gy + n_y + j, n_y))
+    devices = {o: at_offset(*o) for o in THIRD}
+    for device in devices.values():
         pl.semaphore_signal(barrier, inc=1, device_id=device, device_id_type=MESH)
-    pl.semaphore_wait(barrier, len(WINDOW))
+    pl.semaphore_wait(barrier, len(THIRD))
 
     tile = (ROWS, lanes)
     row_at = lax.broadcasted_iota(jnp.int32, tile, 0)
@@ -96,7 +110,7 @@
     done = [0]
 
     def exchange(parts):
-        slot = done[0] % 2
+        slot = done[0] % 3
         done[0] += 1
         copies = []
         for i in (2, 3, 0, 1):
@@ -118,15 +132,27 @@
 
         return wait
 
-    def gather(source, target, send, recv):
+    def remote(source, target, send, recv, offset):
+        copy = pltpu.make_async_remote_copy(
+            src_ref=source,
+            dst_ref=target,
+            send_sem=send,
+            recv_sem=recv,
+            device_id=devices[offset],
+            device_id_type=MESH,
+        )
+        copy.start()
+        return copy
+
+    def gather(offsets, source_of, target, send, recv):
         copies = []
-        for n, device in enumerate(around):
+        for n, (i, j) in enumerate(offsets):
             copy = pltpu.make_async_remote_copy(
-                src_ref=source,
+                src_ref=source_of((i, j)),
                 dst_ref=target.at[n],
                 send_sem=send.at[n],
                 recv_sem=recv.at[n],
-                device_id=device,
+                device_id=devices[(-i, -j)],
                 device_id_type=MESH,
             )
             copy.start()
@@ -201,9 +227,7 @@
 
     each(NX[0], cross_faces)
 
-    def finish_level(level):
-        w, r, span = weights[level], reaction[level], 1 << level
-
+    def finish(w, r, diagonal, inv, count):
         def body(x):
             m = [[r[x, 3 * col + row] for col in range(3)] for row in range(3)]
             for c in range(3):
@@ -211,7 +235,7 @@
                 for k in range(1, 6):
                     total = total + w[x, 3 * k + c]
                 m[c][c] = m[c][c] + total
-                diag[level][x, c] = m[c][c]
+                diagonal[x, c] = m[c][c]
 
             def cofactor(i, j):
                 i1, i2, j1, j2 = (i + 1) % 3, (i + 2) % 3, (j + 1) % 3, (j + 2) % 3
@@ -222,9 +246,12 @@
             scale = OMEGA / det
             for i in range(3):
                 for j in range(3):
-                    inverse[level][x, 3 * i + j] = cof[j][i] * scale
-
-        each(NX[level], body)
+                    inv[x, 3 * i + j] = cof[j][i] * scale
+
+        each(count, body)
+
+    def finish_level(level):
+        finish(weights[level], reaction[level], diag[level], inverse[level], NX[level])
 
     def mask_level(level):
         w, span, last = weights[level], 1 << level, NX[level] - 1
@@ -287,66 +314,87 @@
         each(NX[level + 1], body)
 
     slot_at = lane_at & (SLOTS - 1)
-    cells = [(-i, -j) for i, j in WINDOW] + [(0, 0)]
-
-    def columns(row_of):
-        for t in range(2 * RADIUS + 1):
-            packed = jnp.zeros(tile, jnp.float32)
-            for n, (i, j) in enumerate(cells):
-                if j + RADIUS == t:
-                    packed = jnp.where(row_at == i + RADIUS, wide(row_of(n)), packed)
-            yield t, packed
+    x_at, y_at = row_at + (gx - RADIUS), slot_at + (gy - RADIUS)
+    x_last = jnp.logical_or(x_at == n_x - 1, x_at == -1)
+    x_first = jnp.logical_or(x_at == 0, x_at == n_x)
+    y_last = jnp.logical_or(y_at == n_y - 1, y_at == -1)
+    y_first = jnp.logical_or(y_at == 0, y_at == n_y)
+    z_last, z_first = lane_at >= lanes - SLOTS, lane_at < SLOTS
+    offs = (x_last, x_first, y_last, y_first, z_last, z_first)
+    bits = (2, 2, 1, 1, 4, 4)
+
+    def transposed(tiles):
+        tiles = list(tiles)
+        for bit in (1, 2, 4):
+            clear = (slot_at & bit) == 0
+            for p in range(SLOTS):
+                if not p & bit:
+                    one, two = tiles[p], tiles[p | bit]
+                    tiles[p] = jnp.where(clear, one, along(two, bit))
+                    tiles[p | bit] = jnp.where(clear, along(one, -bit), two)
+        return tiles
+
+    def unpacked(offsets, row_of, own, fill=0.0):
+        tiles = [jnp.full(tile, fill) for _ in range(SLOTS)]
+        for n, (i, j) in enumerate(list(offsets) + OWN):
+            if min(i, j) >= -RADIUS:
+                row = row_of(n) if n < len(offsets) else own
+                tiles[j + RADIUS] = jnp.where(row_at == i + RADIUS, wide(row), tiles[j + RADIUS])
+        return transposed(tiles)
+
+    def child_row(f, x0, c):
+        which = slot_at & 3
+        rows = [wide(f[x0 + p // 2, c, 4 * (p % 2) : 4 * (p % 2) + 1, :]) for p in range(4)]
+        packed = jnp.where(which == 0, rows[0], jnp.where(which == 1, rows[1], jnp.where(which == 2, rows[2], rows[3])))
+        return packed[0:1, :]
+
+    def slot_row(values):
+        packed = values[0]
+        for i in range(1, len(values)):
+            packed = jnp.where(slot_at == i, values[i], packed)
+        return packed
 
     def send_coefficients():
+        for i in range(27):
+            mid_send[i] = child_row(weights[2] if i < 18 else reaction[2], 0, i if i < 18 else i - 18)
         fields_ = [w_own[0, i] for i in range(18)] + [r_own[0, i] for i in range(9)]
         for row in range(4):
-            part = fields_[SLOTS * row : SLOTS * row + SLOTS]
-            packed = part[0]
-            for i in range(1, len(part)):
-                packed = jnp.where(slot_at == i, part[i], packed)
-            coef_send[row : row + 1, :] = packed[0:1, :]
-        return gather(coef_send, coef_recv, coef_send_sem, coef_recv_sem)
-
-    def take_coefficients():
+            low_send[row : row + 1, :] = slot_row(fields_[SLOTS * row : SLOTS * row + SLOTS])[0:1, :]
+        first = gather(INNER, lambda o: mid_send, mid_recv, mid_send_sem, mid_recv_sem)
+        second = gather(FOURTH, lambda o: low_send, low_recv, low_send_sem, low_recv_sem)
+        return first, second
+
+    def take_coefficients(waits):
+        for wait in waits:
+            wait()
+        for i in range(27):
+            made = unpacked(INNER, lambda n: mid_recv[n, i], mid_send[i], 1.0 if i in (18, 22, 26) else 0.0)
+            for p in range(SLOTS):
+                if i < 18:
+                    w_wide[p, i] = made[p]
+                else:
+                    r_wide[p, i - 18] = made[p]
+        finish(w_wide, r_wide, diag_wide, inverse_wide, SLOTS)
+        for k in range(6):
+            for p in range(SLOTS):
+                if ((p & bits[k]) != 0) == (k % 2 == 0):
+                    for c in range(3):
+                        w_wide[p, 3 * k + c] = jnp.where(offs[k], 0.0, w_wide[p, 3 * k + c])
         top = LEVELS - 1
         w, r = weights[top], reaction[top]
         for row in range(4):
-            row_of = lambda n: coef_recv[n, row : row + 1, :] if n < len(WINDOW) else coef_send[row : row + 1, :]
-            count = min(SLOTS, 27 - SLOTS * row)
-            made = [jnp.full(tile, 1.0 if SLOTS * row + i in (18, 22, 26) else 0.0) for i in range(count)]
-            for t, packed in columns(row_of):
-                for i in range(count):
-                    made[i] = jnp.where(slot_at == t, along(packed, t - i), made[i])
-            for i in range(count):
-                at = SLOTS * row + i
-                if at < 18:
-                    w[0, at] = made[i]
-                else:
-                    r[0, at - 18] = made[i]
+            here = slice(row, row + 1)
+            made = unpacked(FOURTH, lambda n: low_recv[n, here, :], low_send[here, :])
+            for p in range(SLOTS):
+                i = SLOTS * row + p
+                if i < 18:
+                    w[0, i] = made[p]
+                elif i < 27:
+                    r[0, i - 18] = made[p]
         finish_level(top)
-        x_at, y_at = row_at + (gx - RADIUS), slot_at + (gy - RADIUS)
-        offs = (
-            jnp.logical_or(x_at == n_x - 1, x_at == -1),
-            jnp.logical_or(x_at == 0, x_at == n_x),
-            jnp.logical_or(y_at == n_y - 1, y_at == -1),
-            jnp.logical_or(y_at == 0, y_at == n_y),
-            lane_at >= lanes - SLOTS,
-            lane_at < SLOTS,
-        )
-        for k, off in enumerate(offs):
-            for c in range(3):
-                w[0, 3 * k + c] = jnp.where(off, 0.0, w[0, 3 * k + c])
-
-    def share_cells(which, values):
-        packed = jnp.where(slot_at == 0, values[0], jnp.where(slot_at == 1, values[1], values[2]))
-        cell_send[which] = packed[0:1, :]
-        gather(cell_send.at[which], cell_recv.at[which], cell_send_sem, cell_recv_sem.at[which])()
-        made = [jnp.zeros(tile, jnp.float32) for _ in range(3)]
-        row_of = lambda n: cell_recv[which, n] if n < len(WINDOW) else cell_send[which]
-        for t, packed in columns(row_of):
-            for c in range(3):
-                made[c] = jnp.where(slot_at == t, along(packed, t - c), made[c])
-        return made
+        for k in range(6):
+            for c in range(3):
+                w[0, 3 * k + c] = jnp.where(offs[k], 0.0, w[0, 3 * k + c])
 
     def spread(value, t):
         value = jnp.where(slot_at == t, value, 0.0)
@@ -354,37 +402,273 @@
             value = value + along(value, -bit if t & bit else bit)
         return value
 
-    def window_sweep(b, u):
+    def wide_residual(p, u):
+        left = []
+        for c in range(3):
+            value = b_wide[p, c] - diag_wide[p, c] * u[p][c]
+            for k in range(6):
+                bit, ahead = bits[k], k % 2 == 0
+                near = u[p ^ bit][c]
+                if ((p & bit) != 0) == ahead:
+                    turn = -1 if ahead else 1
+                    near = down(near, turn) if k < 2 else along(near, turn if k < 4 else turn * SLOTS)
+                value = value + w_wide[p, 3 * k + c] * near
+            for d in range(3):
+                if d != c:
+                    value = value - r_wide[p, 3 * d + c] * u[p][d]
+            left.append(value)
+        return left
+
+    def apply_inverse(v, x, r):
+        return [v[x, 3 * c] * r[0] + v[x, 3 * c + 1] * r[1] + v[x, 3 * c + 2] * r[2] for c in range(3)]
+
+    def wide_fields():
+        return [[u_wide[p, c] for c in range(3)] for p in range(SLOTS)]
+
+    def window_sweep(b, u, patches=None):
         top = LEVELS - 1
         w, r = weights[top], reaction[top]
         left = []
         for c in range(3):
             value = b[c] - diag[top][0, c] * u[c]
-            near = (down(u[c], -1), down(u[c], 1), along(u[c], -1), along(u[c], 1), along(u[c], -SLOTS), along(u[c], SLOTS))
+            before_x, before_y = down(u[c], 1), along(u[c], 1)
+            if patches is not None:
+                before_x = jnp.where(row_at == 0, patches[0][c], before_x)
+                before_y = jnp.where(slot_at == 0, patches[1][c], before_y)
+            near = (down(u[c], -1), before_x, along(u[c], -1), before_y, along(u[c], -SLOTS), along(u[c], SLOTS))
             for k in range(6):
                 value = value + w[0, 3 * k + c] * near[k]
             for d in range(3):
                 if d != c:
                     value = value - r[0, 3 * d + c] * u[d]
             left.append(value)
-        step = solve(top, 0, left)
+        step = apply_inverse(inverse[top], 0, left)
         return [u[c] + step[c] for c in range(3)]
 
-    def coarsest(own):
-        b = share_cells(0, own)
-        u = solve(LEVELS - 1, 0, b)
-        for _ in range(RADIUS):
+    def lower(turn, beside_p, beside_q):
+        for c in range(3):
+            mid_cell[0, c] = child_row(sources[2], 0, c)
+            mid_cell[1, c] = child_row(fields[2].at[0], 1, c)
+        near = INNER + OUTER
+        wait = gather(
+            near, lambda o: mid_cell.at[0 if o in INNER else 1], mid_cells.at[turn], p_send, p_recv.at[turn]
+        )
+        beside_p()
+        wait()
+        for c in range(3):
+            made = unpacked(near, lambda n: mid_cells[turn, n, c], mid_cell[0, c])
+            for p in range(SLOTS):
+                b_wide[p, c] = made[p]
+        inner = jnp.abs(row_at - RADIUS) + jnp.abs(slot_at - RADIUS) <= 2
+        for p in range(SLOTS):
+            b = [b_wide[p, c] for c in range(3)]
+            first = apply_inverse(inverse_wide, p, b)
+            for c in range(3):
+                u_wide[p, c] = jnp.where(inner, first[c], b[c])
+        u_mid = wide_fields()
+        b = [jnp.zeros(tile, jnp.float32) for _ in range(3)]
+        for p in range(SLOTS):
+            left = wide_residual(p, u_mid)
+            b = [b[c] + left[c] for c in range(3)]
+        u = apply_inverse(inverse[LEVELS - 1], 0, b)
+        for _ in range(2):
             u = window_sweep(b, u)
-        u = [spread(value, RADIUS) for value in u]
-        u = share_cells(1, [value[RADIUS : RADIUS + 1, :] for value in u])
-        for _ in range(COARSE_SWEEPS - 1 - RADIUS):
+        row = slot_row([spread(value, RADIUS) for value in u + b])
+        low_cell[0] = row[RADIUS : RADIUS + 1, :]
+        wait = gather(THIRD, lambda o: low_cell.at[0], low_cells.at[turn], q_send, q_recv.at[turn])
+        beside_q()
+        wait()
+        made = unpacked(THIRD, lambda n: low_cells[turn, n], low_cell[0])
+        u, b = made[:3], made[3:6]
+        before_x = [jnp.zeros(tile, jnp.float32) for _ in range(3)]
+        last_y = jnp.zeros(tile, jnp.float32)
+        for n, (i, j) in enumerate(THIRD):
+            if i < -RADIUS:
+                for c in range(3):
+                    value = along(wide(low_cells[turn, n]), j + RADIUS - c)
+                    before_x[c] = jnp.where(slot_at == j + RADIUS, value, before_x[c])
+            if j < -RADIUS:
+                last_y = jnp.where(row_at == i + RADIUS, wide(low_cells[turn, n]), last_y)
+        before_y = [along(last_y, -c) for c in range(3)]
+        u = window_sweep(b, u, (before_x, before_y))
+        for _ in range(COARSE_SWEEPS - 4):
             u = window_sweep(b, u)
-        for c in range(3):
-            for j in range(3):
-                e_rows[c, j] = spread(u[c], RADIUS - 1 + j)
-
-    def e_at(c, i, j):
-        return wide(e_rows[c, 1 + j, RADIUS + i : RADIUS + i + 1, :])
+        u_mid = [[u_wide[p, c] + u[c] for c in range(3)] for p in range(SLOTS)]
+        last = []
+        for p in range(SLOTS):
+            step = apply_inverse(inverse_wide, p, wide_residual(p, u_mid))
+            last.append([u_mid[p][c] + step[c] for c in range(3)])
+        for c in range(3):
+            for x in range(2):
+                for at, (t, y) in enumerate(((RADIUS - 1, 1), (RADIUS, 0), (RADIUS, 1), (RADIUS + 1, 0))):
+                    low, high = last[2 * x + y][c], last[4 + 2 * x + y][c]
+                    if t & 4:
+                        value = jnp.where(slot_at == t, high, 0.0) + along(jnp.where(slot_at == t, low, 0.0), -4)
+                    else:
+                        value = jnp.where(slot_at == t, low, 0.0) + along(jnp.where(slot_at == t, high, 0.0), 4)
+                    for bit in (1, 2):
+                        value = value + along(value, -bit if t & bit else bit)
+                    e_rows[x, at, c] = value
+
+    def mid_at(c, x, y):
+        row = RADIUS + (x // 2)
+        return wide(e_rows[x % 2, y + 1, c, row : row + 1, :])
+
+    odd = (lane_at & 1) != 0
+
+    def even_part(v):
+        return jnp.where(odd, along(v, 1), v)
+
+    def odd_part(v):
+        return jnp.where(odd, v, along(v, -1))
+
+    def rows_tile(rows):
+        made = jnp.zeros(tile, jnp.float32)
+        for at, value in rows:
+            made = jnp.where(row_at == at, wide(value), made)
+        return made
+
+    def pair_up():
+        for x in range(4):
+            for j in range(14):
+                part = [weights[1][x, i] if i < 18 else reaction[1][x, i - 18] for i in (2 * j, 2 * j + 1) if i < 27]
+                coef_own[x, j] = jnp.where(odd, part[-1], part[0])
+        for side, y in ((0, 6), (1, 0)):
+            for j in range(0, 14, 2):
+                rows = [(4 * i + x, coef_own[x, j + i, y : y + 1, :]) for i in range(2) for x in range(4)]
+                coef_y_send[side, j // 2] = rows_tile(rows)
+
+    def send_ring_coefficients():
+        copies = []
+        for side, turn in ((0, 1), (1, -1)):
+            sems = lambda n: (coef_send_sem.at[n], coef_recv_sem.at[n])
+            copies.append(remote(coef_y_send.at[side], coef_y.at[side], *sems(side), (0, turn)))
+            copies.append(remote(coef_own.at[3 - 3 * side], coef_x.at[side], *sems(2 + side), (turn, 0)))
+        return copies
+
+    def take_ring_coefficients(copies):
+        for copy in copies:
+            copy.wait()
+        for p in range(6):
+            edge = 2 if p in (0, 5) else 1
+            filled = jnp.logical_and(row_at >= edge, row_at < ROWS - edge)
+            for j in range(14):
+                if p in (0, 5):
+                    rows = [(2 + k, coef_x[p // 5, j, 2 * k : 2 * k + 1, :]) for k in range(4)]
+                else:
+                    x = p - 1
+                    rows = [(2 + k, coef_own[x, j, 2 * k : 2 * k + 1, :]) for k in range(4)]
+                    at = 4 * (j % 2) + x
+                    rows += [(1, coef_y[0, j // 2, at : at + 1, :]), (6, coef_y[1, j // 2, at : at + 1, :])]
+                both = rows_tile(rows)
+                for i, value in ((2 * j, even_part(both)), (2 * j + 1, odd_part(both))):
+                    if i < 18:
+                        ring_w[p, i] = value
+                    elif i < 27:
+                        ring_r[p, i - 18] = jnp.where(filled, value, 1.0) if i in (18, 22, 26) else value
+        finish(ring_w, ring_r, ring_diag, ring_inverse, 6)
+        off_high = jnp.logical_and(row_at == 5, is_high_y)
+        off_low = jnp.logical_and(row_at == 2, is_low_y)
+        for c in range(3):
+            ring_w[4, c] = jnp.where(is_high_x, 0.0, ring_w[4, c])
+            ring_w[1, 3 + c] = jnp.where(is_low_x, 0.0, ring_w[1, 3 + c])
+
+        def body(p):
+            for k, off in ((2, off_high), (3, off_low), (4, lane_at >= lanes - 2), (5, lane_at < 2)):
+                for c in range(3):
+                    ring_w[p, 3 * k + c] = jnp.where(off, 0.0, ring_w[p, 3 * k + c])
+
+        each(6, body)
+
+    def send_pairs(turn):
+        for x in range(4):
+            for c in range(3):
+                pair_own[x, c] = jnp.where(odd, sources[1][x, c], fields[1][0, x + 1, c])
+        for side, y in ((0, 4), (1, 0)):
+            for c in range(3):
+                rows = [(2 * x + k, pair_own[x, c, y + 2 * k : y + 2 * k + 1, :]) for x in range(4) for k in range(2)]
+                pair_y_send[side, c] = rows_tile(rows)
+        for sx in range(2):
+            for sy in range(2):
+                x, y = 3 - 3 * sx, 6 - 6 * sy
+                for c in range(3):
+                    pair_corner_send[2 * sx + sy, c : c + 1, :] = pair_own[x, c, y : y + 1, :]
+        copies = []
+        sems = lambda n: (pair_send_sem.at[n], pair_recv_sem.at[turn, n])
+        for side, to in ((0, 1), (1, -1)):
+            copies.append(remote(pair_y_send.at[side], pair_y.at[turn, side], *sems(side), (0, to)))
+            source = pair_own.at[pl.ds(2 - 2 * side, 2)]
+            copies.append(remote(source, pair_x.at[turn, side], *sems(2 + side), (to, 0)))
+        for sx in range(2):
+            for sy in range(2):
+                n = 2 * sx + sy
+                to = (1 - 2 * sx, 1 - 2 * sy)
+                copies.append(remote(pair_corner_send.at[n], pair_corner.at[turn, n], *sems(4 + n), to))
+        return copies
+
+    def take_pairs(turn, copies):
+        for copy in copies:
+            copy.wait()
+        for p in range(8):
+            for c in range(3):
+                if 2 <= p < 6:
+                    x = p - 2
+                    rows = [(2 + k, pair_own[x, c, 2 * k : 2 * k + 1, :]) for k in range(4)]
+                    for side in range(2):
+                        for k in range(2):
+                            at = 2 * x + k
+                            rows.append((6 * side + k, pair_y[turn, side, c, at : at + 1, :]))
+                else:
+                    side = p // 4
+                    rows = [(2 + k, pair_x[turn, side, p - 6 * side, c, 2 * k : 2 * k + 1, :]) for k in range(4)]
+                    if p in (1, 6):
+                        for sy in range(2):
+                            rows.append((1 + 5 * sy, pair_corner[turn, 2 * side + sy, c : c + 1, :]))
+                both = rows_tile(rows)
+                ring_u[p, c] = even_part(both)
+                if 1 <= p < 7:
+                    ring_b[p - 1, c] = odd_part(both)
+
+    def ring_sweep():
+        def add(p):
+            x = p // 2 - 1
+            for c in range(3):
+                e = jnp.where(row_at < 2, mid_at(c, x, -1), mid_at(c, x, 0))
+                e = jnp.where(row_at < 4, e, jnp.where(row_at < 6, mid_at(c, x, 1), mid_at(c, x, 2)))
+                ring_u[p, c] += e
+
+        for p in range(8):
+            add(p)
+        for p in range(6):
+            u = [ring_u[p + 1, c] for c in range(3)]
+            left = []
+            for c in range(3):
+                value = ring_b[p, c] - ring_diag[p, c] * u[c]
+                near = (ring_u[p + 2, c], ring_u[p, c], down(u[c], -1), down(u[c], 1), along(u[c], -2), along(u[c], 2))
+                for k in range(6):
+                    value = value + ring_w[p, 3 * k + c] * near[k]
+                for d in range(3):
+                    if d != c:
+                        value = value - ring_r[p, 3 * d + c] * u[d]
+                left.append(value)
+            step = apply_inverse(ring_inverse, p, left)
+            for c in range(3):
+                ring_out[p, c] = u[c] + step[c]
+
+    def add_to_finest(at, slot):
+        f = fields[0]
+        for c in range(3):
+            for p in range(6):
+                rows = [wide(ring_out[p, c, 2 + k : 3 + k, :]) for k in range(4)]
+                e = jnp.where(row_at < 2, rows[0], rows[1])
+                e = jnp.where(row_at < 4, e, jnp.where(row_at < 6, rows[2], rows[3]))
+                for x in {0: (-1,), 5: (8,)}.get(p, (2 * p - 2, 2 * p - 1)):
+                    f[at, x + 1, c] += e
+            for side, row in ((0, 1), (1, 6)):
+                rows = [wide(ring_out[1 + k, c, row : row + 1, :]) for k in range(4)]
+                e = jnp.where(row_at < 2, rows[0], rows[1])
+                e = jnp.where(row_at < 4, e, jnp.where(row_at < 6, rows[2], rows[3]))
+                rows_halo[slot, side, c] += e
 
     def source(level, x):
         if level == 0:
@@ -396,51 +680,23 @@
         return [v[x, 3 * c] * r[0] + v[x, 3 * c + 1] * r[1] + v[x, 3 * c + 2] * r[2] for c in range(3)]
 
     def share(level, at, beside_it=lambda: None):
-        slot, f, count = done[0] % 2, fields[level], NX[level]
-        if level < 2:
-            for side, row in ((0, ROWS - 1), (1, 0)):
-                for c in range(3):
-                    packed = wide(f[at, 1, c, row : row + 1, :])
-                    for x in range(1, count):
-                        packed = jnp.where(row_at == x, wide(f[at, x + 1, c, row : row + 1, :]), packed)
-                    send_y[side, c] = packed
-            wait = exchange(
-                [
-                    (f.at[at, count], f.at[at, 0]),
-                    (f.at[at, 1], f.at[at, count + 1]),
-                    (send_y.at[0], rows_halo.at[slot, 0]),
-                    (send_y.at[1], rows_halo.at[slot, 1]),
-                ]
-            )
-            beside_it()
-            wait()
-            return slot
+        slot, f, count = done[0] % 3, fields[level], NX[level]
         for side, row in ((0, ROWS - 1), (1, 0)):
-            packed = wide(f[at, 1, 0, row : row + 1, :])
-            for x in range(count):
-                for c in range(3):
-                    packed = jnp.where(row_at == 4 * x + c, wide(f[at, x + 1, c, row : row + 1, :]), packed)
-            send_y[side, 0] = packed
-        for side, x in ((0, count), (1, 1)):
-            by_four = row_at & 3
-            packed = jnp.where(by_four == 0, f[at, x, 0], jnp.where(by_four == 1, f[at, x, 1], f[at, x, 2]))
-            send_x[side] = packed
+            for c in range(3):
+                packed = wide(f[at, 1, c, row : row + 1, :])
+                for x in range(1, count):
+                    packed = jnp.where(row_at == x, wide(f[at, x + 1, c, row : row + 1, :]), packed)
+                send_y[side, c] = packed
         wait = exchange(
             [
-                (send_x.at[0], recv_x.at[slot, 0]),
-                (send_x.at[1], recv_x.at[slot, 1]),
-                (send_y.at[0, 0], rows_halo.at[slot, 0, 0]),
-                (send_y.at[1, 0], rows_halo.at[slot, 1, 0]),
+                (f.at[at, count], f.at[at, 0]),
+                (f.at[at, 1], f.at[at, count + 1]),
+                (send_y.at[0], rows_halo.at[slot, 0]),
+                (send_y.at[1], rows_halo.at[slot, 1]),
             ]
         )
         beside_it()
         wait()
-        for side, x in ((0, 0), (1, count + 1)):
-            for c in range(3):
-                value = wide(recv_x[slot, side, c : c + 1, :])
-                if level == 2:
-                    value = jnp.where(row_at < 4, value, wide(recv_x[slot, side, 4 + c : 5 + c, :]))
-                f[at, x, c] = value
         return slot
 
     def residual(level, at, slot, x):
@@ -449,10 +705,7 @@
         b = source(level, x)
         left = []
         for c in range(3):
-            if level < 2:
-                row_high, row_low = (rows_halo[slot, side, c, pl.ds(x, 1), :] for side in (1, 0))
-            else:
-                row_high, row_low = (rows_halo[slot, side, 0, pl.ds(4 * x + c, 1), :] for side in (1, 0))
+            row_high, row_low = (rows_halo[slot, side, c, pl.ds(x, 1), :] for side in (1, 0))
             near = (
                 f[at, x + 2, c],
                 f[at, x, c],
@@ -489,9 +742,6 @@
         def body(x):
             left = [residual(level, at, slot, 2 * x + i)[1] for i in range(2)]
             total = [lanes_(rows(left[0][c] + left[1][c])) for c in range(3)]
-            if level == LEVELS - 2:
-                coarsest(total)
-                return
             first = solve(level + 1, x, total)
             for c in range(3):
                 sources[level + 1][x, c] = total[c]
@@ -499,31 +749,20 @@
 
         each(NX[level + 1], body)
 
-    def cycle(level, at, besides, last=False):
-        f = fields[level]
-        slot = share(level, at, besides[level])
-        restrict(level, at, slot)
-        if level == LEVELS - 2:
-            for c in range(3):
-                own = e_at(c, 0, 0)
-                f[at, 0, c] += e_at(c, -1, 0)
-                f[at, 1, c] += own
-                f[at, 2, c] += own
-                f[at, 3, c] += e_at(c, 1, 0)
-            for side in range(2):
-                step = [e_at(c, 0, 2 * side - 1) for c in range(3)]
-                by_four = row_at & 3
-                rows_halo[slot, side, 0] += jnp.where(by_four == 0, step[0], jnp.where(by_four == 1, step[1], step[2]))
-            return sweep(level, at, slot)
-        e = cycle(level + 1, 0, besides)
-
-        def add(x):
-            for c in range(3):
-                for i in range(2):
-                    f[at, 2 * x + 1 + i, c] += fields[level + 1][e, x + 1, c]
-
-        each(NX[level + 1], add)
-        return sweep(level, at, share(level, at), last)
+    def cycle(at, turn, besides, last=False):
+        slot = share(0, at, besides[0])
+        restrict(0, at, slot)
+        pairs = []
+
+        def beside():
+            pairs.extend(send_pairs(turn))
+            besides[1]()
+
+        restrict(1, 0, share(1, 0, beside))
+        lower(turn, besides[2], lambda: take_pairs(turn, pairs))
+        ring_sweep()
+        add_to_finest(at, slot)
+        return sweep(0, at, slot, last)
 
     def start(x):
         for c, value in enumerate(solve(0, x, source(0, x))):
@@ -532,27 +771,27 @@
     finish_level(0)
     loads["grad"].wait()
     each(NX[0], start)
-    pending = []
+    pending, ring_pending = [], []
 
     def make_levels():
         coarsen(0)
         mask_level(0)
         finish_level(1)
         coarsen(1)
-        mask_level(1)
         finish_level(2)
         coarsen(2)
-        mask_level(2)
-        pending.append(send_coefficients())
-
-    def take():
-        pending[0]()
-        take_coefficients()
+        pending.extend(send_coefficients())
+        pair_up()
+        mask_level(1)
+
+    def take_wide():
+        ring_pending.extend(send_ring_coefficients())
+        take_coefficients(pending)
 
     nothing = lambda: None
-    at = cycle(0, 0, (make_levels, take, nothing))
+    at = cycle(0, 0, (make_levels, take_wide, lambda: take_ring_coefficients(ring_pending)))
     at = sweep(0, at, share(0, at))
-    cycle(0, at, (nothing,) * 3, last=True)
+    cycle(at, 1, (nothing,) * 3, last=True)
 
 
 def local(counts, gradient, potential, coupling, region, contact, rates):
@@ -564,26 +803,58 @@
         scratch += [pltpu.VMEM((n, parts) + tile, f32) for n in NX]
     scratch += [pltpu.VMEM((n, 3) + tile, f32) for n in NX[1:]]
     scratch += [pltpu.VMEM((2, n + 2, 3) + tile, f32) for n in NX]
-    wide_window = len(WINDOW)
     scratch += [
-        pltpu.VMEM((2, 2, 3) + tile, f32),
+        pltpu.VMEM((3, 2, 3) + tile, f32),
         pltpu.VMEM((2,) + tile, f32),
         pltpu.VMEM((2, 3) + tile, f32),
-        pltpu.VMEM((2,) + tile, f32),
-        pltpu.VMEM((2, 2) + tile, f32),
         pltpu.SemaphoreType.DMA((4,)),
-        pltpu.SemaphoreType.DMA((2, 4)),
+        pltpu.SemaphoreType.DMA((3, 4)),
         pltpu.VMEM((1, 18) + tile, f32),
         pltpu.VMEM((1, 9) + tile, f32),
+        pltpu.VMEM((SLOTS, 18) + tile, f32),
+        pltpu.VMEM((SLOTS, 9) + tile, f32),
+        pltpu.VMEM((SLOTS, 3) + tile, f32),
+        pltpu.VMEM((SLOTS, 9) + tile, f32),
+        pltpu.VMEM((SLOTS, 3) + tile, f32),
+        pltpu.VMEM((SLOTS, 3) + tile, f32),
+        pltpu.VMEM((2, 4, 3) + tile, f32),
+        pltpu.VMEM((27, 1, nz), f32),
+        pltpu.VMEM((len(INNER), 27, 1, nz), f32),
         pltpu.VMEM((4, nz), f32),
-        pltpu.VMEM((wide_window, 4, nz), f32),
-        pltpu.VMEM((2, 1, nz), f32),
-        pltpu.VMEM((2, wide_window, 1, nz), f32),
-        pltpu.VMEM((3, 3) + tile, f32),
-        pltpu.SemaphoreType.DMA((wide_window,)),
-        pltpu.SemaphoreType.DMA((wide_window,)),
-        pltpu.SemaphoreType.DMA((wide_window,)),
-        pltpu.SemaphoreType.DMA((2, wide_window)),
+        pltpu.VMEM((len(FOURTH), 4, nz), f32),
+        pltpu.VMEM((2, 3, 1, nz), f32),
+        pltpu.VMEM((2, len(INNER + OUTER), 3, 1, nz), f32),
+        pltpu.VMEM((1, 1, nz), f32),
+        pltpu.VMEM((2, len(THIRD), 1, nz), f32),
+        pltpu.SemaphoreType.DMA((len(INNER),)),
+        pltpu.SemaphoreType.DMA((len(INNER),)),
+        pltpu.SemaphoreType.DMA((len(FOURTH),)),
+        pltpu.SemaphoreType.DMA((len(FOURTH),)),
+        pltpu.SemaphoreType.DMA((len(INNER + OUTER),)),
+        pltpu.SemaphoreType.DMA((2, len(INNER + OUTER))),
+        pltpu.SemaphoreType.DMA((len(THIRD),)),
+        pltpu.SemaphoreType.DMA((2, len(THIRD))),
+        pltpu.VMEM((8, 3) + tile, f32),
+        pltpu.VMEM((6, 3) + tile, f32),
+        pltpu.VMEM((6, 18) + tile, f32),
+        pltpu.VMEM((6, 9) + tile, f32),
+        pltpu.VMEM((6, 3) + tile, f32),
+        pltpu.VMEM((6, 9) + tile, f32),
+        pltpu.VMEM((6, 3) + tile, f32),
+        pltpu.VMEM((4, 3) + tile, f32),
+        pltpu.VMEM((2, 2, 2, 3) + tile, f32),
+        pltpu.VMEM((2, 3) + tile, f32),
+        pltpu.VMEM((2, 2, 3) + tile, f32),
+        pltpu.VMEM((4, 4, nz), f32),
+        pltpu.VMEM((2, 4, 4, nz), f32),
+        pltpu.SemaphoreType.DMA((8,)),
+        pltpu.SemaphoreType.DMA((2, 8)),
+        pltpu.VMEM((4, 14) + tile, f32),
+        pltpu.VMEM((2, 14) + tile, f32),
+        pltpu.VMEM((2, 7) + tile, f32),
+        pltpu.VMEM((2, 7) + tile, f32),
+        pltpu.SemaphoreType.DMA((4,)),
+        pltpu.SemaphoreType.DMA((4,)),
         pltpu.VMEM(gradient.shape, f32),
         pltpu.VMEM((10,) + tile, f32),
         pltpu.VMEM(coupling.shape, f32),

time: 94.2 us -> 75.5 us (0.80)
  Pallas kernels: 92.5 us -> 73.8 us
    pallas_call x1, Pallas kernels: 92.5 us -> 73.8 us  [local(): pl.pallas_call(functools.partial(kernel, counts), out_shape=jax.ShapeDtyp...]
where the time goes in v3:
time: 75.5 us; the launch traced here: 75.4 us
  Pallas kernels  73.8 us (98%)
  local copies, waits for them, and re-layouts  1.62 us (2%)
    pallas_call x1, Pallas kernels, local(): pl.pallas_call(functools.partial(kernel, counts), out_shape=jax.ShapeDtyp...  73.8 us
    unnamed x1, local copies, waits for them, and re-layouts  1.62 us

profile of v3, /device:TPU:1, one launch (start us, length us, event | category | flops | bytes accessed | tf_op | source)
XLA Modules:
  0.0 75.4 jit_solution(4941276799538614573)
XLA Ops:
  0.0 73.8 %shard_map.64 = f32[3,8,8,256]{3,2,1,0:T(8,128)} custom-call(f32[3,8,8,256]{3,2,1,0:T(8,128)} %grad_in.1, f32[8,8,256]{2,1,0:T(8,128)} %pot_in.1, f32[3,3,8,8,256]{4,3,2,1,0:T(8,128)} %coup_in.1, s32[8,8,256]{2,1,0:T(8,128)} %region_in.1, s32[8,8,256]{2,1,0:T(8,128)} %contact_in.1, f32[4,3]{1,0:T(4,128)} %rates_in.1), custom_call_target="tpu_custom_call" | custom-call | tf_op jit(solution)/shard_map/pallas_call | solution.py:867
  73.8 1.6 %copy.8 = f32[3,8,8,256]{3,2,1,0:T(8,128)} copy(f32[3,8,8,256]{3,2,1,0:T(8,128)} %shard_map.64) | data formatting | bytes 393216

commit v4 on v3

--- a/solution.py
+++ b/solution.py
@@ -96,9 +96,9 @@
     barrier = pltpu.get_barrier_semaphore()
     at_offset = lambda i, j: (lax.rem(gx + n_x + i, n_x), lax.rem(gy + n_y + j, n_y))
     devices = {o: at_offset(*o) for o in THIRD}
-    for device in devices.values():
-        pl.semaphore_signal(barrier, inc=1, device_id=device, device_id_type=MESH)
-    pl.semaphore_wait(barrier, len(THIRD))
+    for offset in INNER:
+        pl.semaphore_signal(barrier, inc=1, device_id=devices[offset], device_id_type=MESH)
+    pl.semaphore_wait(barrier, len(INNER))
 
     tile = (ROWS, lanes)
     row_at = lax.broadcasted_iota(jnp.int32, tile, 0)
@@ -145,22 +145,12 @@
         return copy
 
     def gather(offsets, source_of, target, send, recv):
-        copies = []
         for n, (i, j) in enumerate(offsets):
-            copy = pltpu.make_async_remote_copy(
-                src_ref=source_of((i, j)),
-                dst_ref=target.at[n],
-                send_sem=send.at[n],
-                recv_sem=recv.at[n],
-                device_id=devices[(-i, -j)],
-                device_id_type=MESH,
-            )
-            copy.start()
-            copies.append(copy)
+            remote(source_of((i, j)), target.at[n], send, recv, (-i, -j))
 
         def wait():
-            for copy in copies:
-                copy.wait()
+            pltpu.make_async_copy(target, target, send).wait()
+            pltpu.make_async_copy(target, target, recv).wait()
 
         return wait
 
@@ -360,9 +350,10 @@
         fields_ = [w_own[0, i] for i in range(18)] + [r_own[0, i] for i in range(9)]
         for row in range(4):
             low_send[row : row + 1, :] = slot_row(fields_[SLOTS * row : SLOTS * row + SLOTS])[0:1, :]
-        first = gather(INNER, lambda o: mid_send, mid_recv, mid_send_sem, mid_recv_sem)
-        second = gather(FOURTH, lambda o: low_send, low_recv, low_send_sem, low_recv_sem)
-        return first, second
+        return gather(INNER, lambda o: mid_send, mid_recv, mid_send_sem, mid_recv_sem)
+
+    def send_low_coefficients():
+        return gather(FOURTH, lambda o: low_send, low_recv, low_send_sem, low_recv_sem)
 
     def take_coefficients(waits):
         for wait in waits:
@@ -780,11 +771,12 @@
         coarsen(1)
         finish_level(2)
         coarsen(2)
-        pending.extend(send_coefficients())
+        pending.append(send_coefficients())
         pair_up()
         mask_level(1)
 
     def take_wide():
+        pending.append(send_low_coefficients())
         ring_pending.extend(send_ring_coefficients())
         take_coefficients(pending)
 
@@ -826,14 +818,14 @@
         pltpu.VMEM((2, len(INNER + OUTER), 3, 1, nz), f32),
         pltpu.VMEM((1, 1, nz), f32),
         pltpu.VMEM((2, len(THIRD), 1, nz), f32),
-        pltpu.SemaphoreType.DMA((len(INNER),)),
-        pltpu.SemaphoreType.DMA((len(INNER),)),
-        pltpu.SemaphoreType.DMA((len(FOURTH),)),
-        pltpu.SemaphoreType.DMA((len(FOURTH),)),
-        pltpu.SemaphoreType.DMA((len(INNER + OUTER),)),
-        pltpu.SemaphoreType.DMA((2, len(INNER + OUTER))),
-        pltpu.SemaphoreType.DMA((len(THIRD),)),
-        pltpu.SemaphoreType.DMA((2, len(THIRD))),
+        pltpu.SemaphoreType.DMA,
+        pltpu.SemaphoreType.DMA,
+        pltpu.SemaphoreType.DMA,
+        pltpu.SemaphoreType.DMA,
+        pltpu.SemaphoreType.DMA,
+        pltpu.SemaphoreType.DMA((2,)),
+        pltpu.SemaphoreType.DMA,
+        pltpu.SemaphoreType.DMA((2,)),
         pltpu.VMEM((8, 3) + tile, f32),
         pltpu.VMEM((6, 3) + tile, f32),
         pltpu.VMEM((6, 18) + tile, f32),

time: 75.5 us -> 76.1 us (level)
  no operation moved by 1% of the time
where the time goes in v4:
time: 76.1 us; the launch traced here: 76 us
  Pallas kernels  74.4 us (98%)
  local copies, waits for them, and re-layouts  1.62 us (2%)
    pallas_call x1, Pallas kernels, local(): pl.pallas_call(functools.partial(kernel, counts), out_shape=jax.ShapeDtyp...  74.4 us
    unnamed x1, local copies, waits for them, and re-layouts  1.62 us

profile of v4, /device:TPU:1, one launch (start us, length us, event | category | flops | bytes accessed | tf_op | source)
XLA Modules:
  0.0 76.0 jit_solution(13291221245418280359)
XLA Ops:
  0.0 74.4 %shard_map.64 = f32[3,8,8,256]{3,2,1,0:T(8,128)} custom-call(f32[3,8,8,256]{3,2,1,0:T(8,128)} %grad_in.1, f32[8,8,256]{2,1,0:T(8,128)} %pot_in.1, f32[3,3,8,8,256]{4,3,2,1,0:T(8,128)} %coup_in.1, s32[8,8,256]{2,1,0:T(8,128)} %region_in.1, s32[8,8,256]{2,1,0:T(8,128)} %contact_in.1, f32[4,3]{1,0:T(4,128)} %rates_in.1), custom_call_target="tpu_custom_call" | custom-call | tf_op jit(solution)/shard_map/pallas_call | solution.py:859
  74.4 1.6 %copy.8 = f32[3,8,8,256]{3,2,1,0:T(8,128)} copy(f32[3,8,8,256]{3,2,1,0:T(8,128)} %shard_map.64) | data formatting | bytes 393216

commit v5 on v4

--- a/solution.py
+++ b/solution.py
@@ -85,7 +85,7 @@
     mid_send_sem, mid_recv_sem, low_send_sem, low_recv_sem, p_send, p_recv, q_send, q_recv = scratch[45:53]
     ring_u, ring_b, ring_w, ring_r, ring_diag, ring_inverse, ring_out = scratch[53:60]
     pair_own, pair_x, pair_y_send, pair_y, pair_corner_send, pair_corner, pair_send_sem, pair_recv_sem = scratch[60:68]
-    coef_own, coef_x, coef_y_send, coef_y, coef_send_sem, coef_recv_sem = scratch[68:]
+    coef_own, coef_x, coef_y_send, coef_y, coef_send_sem, coef_recv_sem, part = scratch[68:]
     n_x, n_y = counts
     lanes = out.shape[-1]
     gx, gy = lax.axis_index("gx"), lax.axis_index("gy")
@@ -347,12 +347,12 @@
     def send_coefficients():
         for i in range(27):
             mid_send[i] = child_row(weights[2] if i < 18 else reaction[2], 0, i if i < 18 else i - 18)
+        return gather(INNER, lambda o: mid_send, mid_recv, mid_send_sem, mid_recv_sem)
+
+    def send_low_coefficients():
         fields_ = [w_own[0, i] for i in range(18)] + [r_own[0, i] for i in range(9)]
         for row in range(4):
             low_send[row : row + 1, :] = slot_row(fields_[SLOTS * row : SLOTS * row + SLOTS])[0:1, :]
-        return gather(INNER, lambda o: mid_send, mid_recv, mid_send_sem, mid_recv_sem)
-
-    def send_low_coefficients():
         return gather(FOURTH, lambda o: low_send, low_recv, low_send_sem, low_recv_sem)
 
     def take_coefficients(waits):
@@ -687,8 +687,42 @@
             ]
         )
         beside_it()
+        inner(level, at)
         wait()
         return slot
+
+    def inner(level, at):
+        f, w, r, span, count = fields[level], weights[level], reaction[level], 1 << level, NX[level]
+        for x in range(count):
+            u = [f[at, x + 1, c] for c in range(3)]
+            b = source(level, x)
+            for c in range(3):
+                value = b[c] - diag[level][x, c] * u[c]
+                value = value + w[x, 6 + c] * jnp.where(row_at >= ROWS - span, 0.0, down(u[c], -span))
+                value = value + w[x, 9 + c] * jnp.where(row_at < span, 0.0, down(u[c], span))
+                value = value + w[x, 12 + c] * along(u[c], -span) + w[x, 15 + c] * along(u[c], span)
+                if x < count - 1:
+                    value = value + w[x, c] * f[at, x + 2, c]
+                if x > 0:
+                    value = value + w[x, 3 + c] * f[at, x, c]
+                for d in range(3):
+                    if d != c:
+                        value = value - r[x, 3 * d + c] * u[d]
+                part[x, c] = value
+
+    def rest(level, at, slot, x):
+        f, w, span, count = fields[level], weights[level], 1 << level, NX[level]
+        left = []
+        for c in range(3):
+            row_high, row_low = (rows_halo[slot, side, c, x : x + 1, :] for side in (1, 0))
+            value = jnp.where(row_at >= ROWS - span, w[x, 6 + c] * wide(row_high), 0.0)
+            value = part[x, c] + jnp.where(row_at < span, w[x, 9 + c] * wide(row_low), value)
+            if x == 0:
+                value = value + w[x, 3 + c] * f[at, 0, c]
+            if x == count - 1:
+                value = value + w[x, c] * f[at, count + 1, c]
+            left.append(value)
+        return [f[at, x + 1, c] for c in range(3)], left
 
     def residual(level, at, slot, x):
         f, w, r, span = fields[level], weights[level], reaction[level], 1 << level
@@ -696,12 +730,11 @@
         b = source(level, x)
         left = []
         for c in range(3):
-            row_high, row_low = (rows_halo[slot, side, c, pl.ds(x, 1), :] for side in (1, 0))
             near = (
                 f[at, x + 2, c],
                 f[at, x, c],
-                jnp.where(row_at >= ROWS - span, wide(row_high), down(u[c], -span)),
-                jnp.where(row_at < span, wide(row_low), down(u[c], span)),
+                jnp.where(row_at >= ROWS - span, wide(rows_halo[slot, 1, c, x : x + 1, :]), down(u[c], -span)),
+                jnp.where(row_at < span, wide(rows_halo[slot, 0, c, x : x + 1, :]), down(u[c], span)),
                 along(u[c], -span),
                 along(u[c], span),
             )
@@ -714,31 +747,26 @@
             left.append(value)
         return u, left
 
-    def sweep(level, at, slot, last=False):
-        def body(x):
-            u, left = residual(level, at, slot, x)
-            step = solve(level, x, left)
+    def sweep(at, slot, left_of, last=False):
+        for x in range(NX[0]):
+            u, left = left_of(0, at, slot, x)
+            step = solve(0, x, left)
             for c in range(3):
                 if last:
                     out[c, x] = u[c] + step[c]
                 else:
-                    fields[level][1 - at, x + 1, c] = u[c] + step[c]
-
-        each(NX[level], body)
+                    fields[0][1 - at, x + 1, c] = u[c] + step[c]
         return 1 - at
 
     def restrict(level, at, slot):
         rows, lanes_ = pair_tools(level)[4:]
-
-        def body(x):
-            left = [residual(level, at, slot, 2 * x + i)[1] for i in range(2)]
+        for x in range(NX[level + 1]):
+            left = [rest(level, at, slot, 2 * x + i)[1] for i in range(2)]
             total = [lanes_(rows(left[0][c] + left[1][c])) for c in range(3)]
             first = solve(level + 1, x, total)
             for c in range(3):
                 sources[level + 1][x, c] = total[c]
                 fields[level + 1][0, x + 1, c] = first[c]
-
-        each(NX[level + 1], body)
 
     def cycle(at, turn, besides, last=False):
         slot = share(0, at, besides[0])
@@ -750,10 +778,15 @@
             besides[1]()
 
         restrict(1, 0, share(1, 0, beside))
-        lower(turn, besides[2], lambda: take_pairs(turn, pairs))
+
+        def beside_q():
+            take_pairs(turn, pairs)
+            besides[3]()
+
+        lower(turn, besides[2], beside_q)
         ring_sweep()
         add_to_finest(at, slot)
-        return sweep(0, at, slot, last)
+        return sweep(at, slot, residual, last)
 
     def start(x):
         for c, value in enumerate(solve(0, x, source(0, x))):
@@ -764,26 +797,34 @@
     each(NX[0], start)
     pending, ring_pending = [], []
 
-    def make_levels():
+    def beside_first():
         coarsen(0)
         mask_level(0)
         finish_level(1)
         coarsen(1)
+        pending.append(send_coefficients())
+
+    def beside_second():
+        pair_up()
+        ring_pending.extend(send_ring_coefficients())
+        mask_level(1)
         finish_level(2)
         coarsen(2)
-        pending.append(send_coefficients())
-        pair_up()
-        mask_level(1)
-
-    def take_wide():
         pending.append(send_low_coefficients())
-        ring_pending.extend(send_ring_coefficients())
-        take_coefficients(pending)
 
     nothing = lambda: None
-    at = cycle(0, 0, (make_levels, take_wide, lambda: take_ring_coefficients(ring_pending)))
-    at = sweep(0, at, share(0, at))
-    cycle(at, 1, (nothing,) * 3, last=True)
+    at = cycle(
+        0,
+        0,
+        (
+            beside_first,
+            beside_second,
+            lambda: take_coefficients(pending),
+            lambda: take_ring_coefficients(ring_pending),
+        ),
+    )
+    at = sweep(at, share(0, at), rest)
+    cycle(at, 1, (nothing,) * 4, last=True)
 
 
 def local(counts, gradient, potential, coupling, region, contact, rates):
@@ -847,6 +888,7 @@
         pltpu.VMEM((2, 7) + tile, f32),
         pltpu.SemaphoreType.DMA((4,)),
         pltpu.SemaphoreType.DMA((4,)),
+        pltpu.VMEM((NX[0], 3) + tile, f32),
         pltpu.VMEM(gradient.shape, f32),
         pltpu.VMEM((10,) + tile, f32),
         pltpu.VMEM(coupling.shape, f32),

time: 76.1 us -> 70.3 us (0.924)
  Pallas kernels: 74.4 us -> 68.6 us
    pallas_call x1, Pallas kernels: 74.4 us -> 68.6 us  [local(): pl.pallas_call(functools.partial(kernel, counts), out_shape=jax.ShapeDtyp...]
where the time goes in v5:
time: 70.3 us; the launch traced here: 70.2 us
  Pallas kernels  68.6 us (98%)
  local copies, waits for them, and re-layouts  1.62 us (2%)
    pallas_call x1, Pallas kernels, local(): pl.pallas_call(functools.partial(kernel, counts), out_shape=jax.ShapeDtyp...  68.6 us
    unnamed x1, local copies, waits for them, and re-layouts  1.62 us

profile of v5, /device:TPU:1, one launch (start us, length us, event | category | flops | bytes accessed | tf_op | source)
XLA Modules:
  0.0 70.2 jit_solution(1490357102485288684)
XLA Ops:
  0.0 68.6 %shard_map.64 = f32[3,8,8,256]{3,2,1,0:T(8,128)} custom-call(f32[3,8,8,256]{3,2,1,0:T(8,128)} %grad_in.1, f32[8,8,256]{2,1,0:T(8,128)} %pot_in.1, f32[3,3,8,8,256]{4,3,2,1,0:T(8,128)} %coup_in.1, s32[8,8,256]{2,1,0:T(8,128)} %region_in.1, s32[8,8,256]{2,1,0:T(8,128)} %contact_in.1, f32[4,3]{1,0:T(4,128)} %rates_in.1), custom_call_target="tpu_custom_call" | custom-call | tf_op jit(solution)/shard_map/pallas_call | solution.py:901
  68.6 1.6 %copy.8 = f32[3,8,8,256]{3,2,1,0:T(8,128)} copy(f32[3,8,8,256]{3,2,1,0:T(8,128)} %shard_map.64) | data formatting | bytes 393216

commit v6 on v5

--- a/solution.py
+++ b/solution.py
@@ -85,7 +85,9 @@
     mid_send_sem, mid_recv_sem, low_send_sem, low_recv_sem, p_send, p_recv, q_send, q_recv = scratch[45:53]
     ring_u, ring_b, ring_w, ring_r, ring_diag, ring_inverse, ring_out = scratch[53:60]
     pair_own, pair_x, pair_y_send, pair_y, pair_corner_send, pair_corner, pair_send_sem, pair_recv_sem = scratch[60:68]
-    coef_own, coef_x, coef_y_send, coef_y, coef_send_sem, coef_recv_sem, part = scratch[68:]
+    coef_own, coef_x, coef_y_send, coef_y, coef_send_sem, coef_recv_sem, part, coef_corner_send, coef_corner = scratch[68:77]
+    rim_w, rim_r, rim_diag, rim_inverse, rim_base, rim_pot, rim_pot_corner_send, rim_pot_corner = scratch[77:85]
+    base, rim_y_send, rim_y, rim_send_sem, rim_recv_sem = scratch[85:]
     n_x, n_y = counts
     lanes = out.shape[-1]
     gx, gy = lax.axis_index("gx"), lax.axis_index("gy")
@@ -535,17 +537,25 @@
             sems = lambda n: (coef_send_sem.at[n], coef_recv_sem.at[n])
             copies.append(remote(coef_y_send.at[side], coef_y.at[side], *sems(side), (0, turn)))
             copies.append(remote(coef_own.at[3 - 3 * side], coef_x.at[side], *sems(2 + side), (turn, 0)))
+        for n in range(4):
+            x, y = 3 - 3 * (n // 2), 6 - 6 * (n % 2)
+            for j in range(14):
+                coef_corner_send[n, j : j + 1, :] = coef_own[x, j, y : y + 1, :]
+            to = (1 - 2 * (n // 2), 1 - 2 * (n % 2))
+            copies.append(
+                remote(coef_corner_send.at[n], coef_corner.at[n], coef_send_sem.at[4 + n], coef_recv_sem.at[4 + n], to)
+            )
         return copies
 
     def take_ring_coefficients(copies):
         for copy in copies:
             copy.wait()
         for p in range(6):
-            edge = 2 if p in (0, 5) else 1
-            filled = jnp.logical_and(row_at >= edge, row_at < ROWS - edge)
+            filled = jnp.logical_and(row_at >= 1, row_at < ROWS - 1)
             for j in range(14):
                 if p in (0, 5):
                     rows = [(2 + k, coef_x[p // 5, j, 2 * k : 2 * k + 1, :]) for k in range(4)]
+                    rows += [(1 + 5 * sy, coef_corner[2 * (p // 5) + sy, j : j + 1, :]) for sy in range(2)]
                 else:
                     x = p - 1
                     rows = [(2 + k, coef_own[x, j, 2 * k : 2 * k + 1, :]) for k in range(4)]
@@ -582,8 +592,10 @@
         for sx in range(2):
             for sy in range(2):
                 x, y = 3 - 3 * sx, 6 - 6 * sy
-                for c in range(3):
-                    pair_corner_send[2 * sx + sy, c : c + 1, :] = pair_own[x, c, y : y + 1, :]
+                for i, (at_x, at_y) in enumerate(((x, y), (2 - sx, y), (x, 4 - 2 * sy))):
+                    for c in range(3):
+                        n = 3 * i + c
+                        pair_corner_send[2 * sx + sy, n : n + 1, :] = pair_own[at_x, c, at_y : at_y + 1, :]
         copies = []
         sems = lambda n: (pair_send_sem.at[n], pair_recv_sem.at[turn, n])
         for side, to in ((0, 1), (1, -1)):
@@ -612,9 +624,11 @@
                 else:
                     side = p // 4
                     rows = [(2 + k, pair_x[turn, side, p - 6 * side, c, 2 * k : 2 * k + 1, :]) for k in range(4)]
-                    if p in (1, 6):
-                        for sy in range(2):
-                            rows.append((1 + 5 * sy, pair_corner[turn, 2 * side + sy, c : c + 1, :]))
+                    for sy in range(2):
+                        cells = ((0, 1 + 5 * sy), (2, 7 * sy)) if p in (1, 6) else ((1, 1 + 5 * sy),)
+                        for i, row in cells:
+                            n = 3 * i + c
+                            rows.append((row, pair_corner[turn, 2 * side + sy, n : n + 1, :]))
                 both = rows_tile(rows)
                 ring_u[p, c] = even_part(both)
                 if 1 <= p < 7:
@@ -660,6 +674,131 @@
                 e = jnp.where(row_at < 2, rows[0], rows[1])
                 e = jnp.where(row_at < 4, e, jnp.where(row_at < 6, rows[2], rows[3]))
                 rows_halo[slot, side, c] += e
+
+    def packed_y(f, at):
+        return rows_tile([(x, f(x)[at : at + 1, :]) for x in range(8)])
+
+    def send_rim():
+        copies = []
+        sems = lambda n: (rim_send_sem.at[n], rim_recv_sem.at[n])
+        for side, to in ((0, 1), (1, -1)):
+            row, second = 7 - 7 * side, 6 - 5 * side
+            for i in range(9):
+                rim_y_send[side, i] = rows_tile([(x, reaction[0][x, i, row : row + 1, :]) for x in range(8)])
+            rim_y_send[side, 9] = rows_tile([(x, pot[x + 1, second : second + 1, :]) for x in range(8)])
+            for c in range(3):
+                rim_y_send[side, 10 + c] = rows_tile([(x, base[x, c, row : row + 1, :]) for x in range(8)])
+            copies.append(remote(rim_y_send.at[side], rim_y.at[side], *sems(side), (0, to)))
+            copies.append(remote(reaction[0].at[row], rim_r.at[side], *sems(2 + side), (to, 0)))
+            copies.append(remote(pot.at[second + 1], rim_pot.at[side], *sems(4 + side), (to, 0)))
+            copies.append(remote(base.at[row], rim_base.at[side], *sems(6 + side), (to, 0)))
+        for n in range(4):
+            x, y = 7 - 7 * (n // 2), 7 - 7 * (n % 2)
+            rim_pot_corner_send[n] = pot[x + 1, y : y + 1, :]
+            to = (1 - 2 * (n // 2), 1 - 2 * (n % 2))
+            copies.append(remote(rim_pot_corner_send.at[n], rim_pot_corner.at[n], *sems(8 + n), to))
+        return copies
+
+    def ordered(t, out_side, in_side, ahead, behind, above, below):
+        across = (in_side, out_side) if t % 2 == 0 else (out_side, in_side)
+        return (across + (ahead, behind) if t < 2 else (ahead, behind) + across) + (above, below)
+
+    def take_rim(copies):
+        for copy in copies:
+            copy.wait()
+        for side in range(2):
+            for i in range(9):
+                rim_r[2 + side, i] = rim_y[side, i]
+            for c in range(3):
+                rim_base[2 + side, c] = rim_y[side, 10 + c]
+        for t in range(4):
+            side = t % 2
+            if t < 2:
+                here, beyond, inside = pot[9 * side], rim_pot[side], pot[1 + 7 * side]
+                first, last = 2 * side, 2 * side + 1
+                edges = (is_low_y, is_high_y)
+            else:
+                here, beyond = pot_y[side], rim_y[side, 9]
+                row = 7 * side
+                inside = rows_tile([(x, pot[x + 1, row : row + 1, :]) for x in range(8)])
+                first, last = side, 2 + side
+                edges = (is_low_x, is_high_x)
+            corner = lambda n, off: jnp.where(off, 0.0, wide(rim_pot_corner[n]))
+            near = ordered(
+                t,
+                beyond,
+                inside,
+                jnp.where(row_at == ROWS - 1, corner(last, edges[1]), down(here, -1)),
+                jnp.where(row_at == 0, corner(first, edges[0]), down(here, 1)),
+                jnp.where(lane_at == lanes - 1, 0.0, along(here, -1)),
+                jnp.where(lane_at == 0, 0.0, along(here, 1)),
+            )
+            for k in range(6):
+                plus, minus = face_weights(here - near[k])
+                rim_w[t, 3 * k] = jnp.ones(tile, jnp.float32)
+                rim_w[t, 3 * k + 1] = plus
+                rim_w[t, 3 * k + 2] = minus
+        finish(rim_w, rim_r, rim_diag, rim_inverse, 4)
+        for t in range(4):
+            ahead, off_high, off_low = (2, is_high_y, is_low_y) if t < 2 else (0, is_high_x, is_low_x)
+            masks = (
+                (ahead, jnp.logical_and(row_at == ROWS - 1, off_high)),
+                (ahead + 1, jnp.logical_and(row_at == 0, off_low)),
+                (4, lane_at == lanes - 1),
+                (5, lane_at == 0),
+            )
+            for k, off in masks:
+                for c in range(3):
+                    rim_w[t, 3 * k + c] = jnp.where(off, 0.0, rim_w[t, 3 * k + c])
+
+    def doubled(rows):
+        e = jnp.where(row_at < 2, wide(rows[0]), wide(rows[1]))
+        return jnp.where(row_at < 4, e, jnp.where(row_at < 6, wide(rows[2]), wide(rows[3])))
+
+    def rim_sweep(at):
+        for t in range(4):
+            side = t % 2
+            e, near = [], []
+            for c in range(3):
+                cell = lambda p, row: ring_out[p, c, row : row + 1, :]
+                if t < 2:
+                    p, p_in = 5 * side, 1 + 3 * side
+                    here = doubled([cell(p, 2 + k) for k in range(4)])
+                    inside = doubled([cell(p_in, 2 + k) for k in range(4)])
+                    first, last = cell(p, 1), cell(p, 6)
+                else:
+                    row, row_in = 1 + 5 * side, 2 + 3 * side
+                    here = doubled([cell(1 + k, row) for k in range(4)])
+                    inside = doubled([cell(1 + k, row_in) for k in range(4)])
+                    first, last = cell(0, row), cell(5, row)
+                e.append(here)
+                near.append(
+                    ordered(
+                        t,
+                        here,
+                        inside,
+                        jnp.where(row_at == ROWS - 1, wide(last), down(here, -1)),
+                        jnp.where(row_at == 0, wide(first), down(here, 1)),
+                        along(here, -1),
+                        along(here, 1),
+                    )
+                )
+            left = []
+            for c in range(3):
+                value = -rim_diag[t, c] * e[c]
+                for k in range(6):
+                    value = value + rim_w[t, 3 * k + c] * near[c][k]
+                for d in range(3):
+                    if d != c:
+                        value = value - rim_r[t, 3 * d + c] * e[d]
+                left.append(value)
+            step = apply_inverse(rim_inverse, t, left)
+            for c in range(3):
+                value = rim_base[t, c] + e[c] + step[c]
+                if t < 2:
+                    fields[0][at, 9 * side, c] = value
+                else:
+                    rows_halo[3, side, c] = value
 
     def source(level, x):
         if level == 0:
@@ -755,13 +894,20 @@
                 if last:
                     out[c, x] = u[c] + step[c]
                 else:
-                    fields[0][1 - at, x + 1, c] = u[c] + step[c]
-        return 1 - at
-
-    def restrict(level, at, slot):
+                    fields[0][at + 1, x + 1, c] = u[c] + step[c]
+        return at + 1
+
+    def restrict(level, at, slot, keep=False):
         rows, lanes_ = pair_tools(level)[4:]
         for x in range(NX[level + 1]):
-            left = [rest(level, at, slot, 2 * x + i)[1] for i in range(2)]
+            left = []
+            for i in range(2):
+                u, r = rest(level, at, slot, 2 * x + i)
+                left.append(r)
+                if keep:
+                    step = solve(level, 2 * x + i, r)
+                    for c in range(3):
+                        base[2 * x + i, c] = u[c] + step[c]
             total = [lanes_(rows(left[0][c] + left[1][c])) for c in range(3)]
             first = solve(level + 1, x, total)
             for c in range(3):
@@ -770,7 +916,7 @@
 
     def cycle(at, turn, besides, last=False):
         slot = share(0, at, besides[0])
-        restrict(0, at, slot)
+        restrict(0, at, slot, keep=not last)
         pairs = []
 
         def beside():
@@ -785,6 +931,8 @@
 
         lower(turn, besides[2], beside_q)
         ring_sweep()
+        if not last:
+            rim_sweep(at + 1)
         add_to_finest(at, slot)
         return sweep(at, slot, residual, last)
 
@@ -795,7 +943,7 @@
     finish_level(0)
     loads["grad"].wait()
     each(NX[0], start)
-    pending, ring_pending = [], []
+    pending, ring_pending, rim_pending = [], [], []
 
     def beside_first():
         coarsen(0)
@@ -811,6 +959,11 @@
         finish_level(2)
         coarsen(2)
         pending.append(send_low_coefficients())
+        rim_pending.extend(send_rim())
+
+    def beside_fourth():
+        take_ring_coefficients(ring_pending)
+        take_rim(rim_pending)
 
     nothing = lambda: None
     at = cycle(
@@ -820,10 +973,10 @@
             beside_first,
             beside_second,
             lambda: take_coefficients(pending),
-            lambda: take_ring_coefficients(ring_pending),
+            beside_fourth,
         ),
     )
-    at = sweep(at, share(0, at), rest)
+    at = sweep(at, 3, residual)
     cycle(at, 1, (nothing,) * 4, last=True)
 
 
@@ -835,9 +988,9 @@
     for parts in (18, 9, 3, 9):
         scratch += [pltpu.VMEM((n, parts) + tile, f32) for n in NX]
     scratch += [pltpu.VMEM((n, 3) + tile, f32) for n in NX[1:]]
-    scratch += [pltpu.VMEM((2, n + 2, 3) + tile, f32) for n in NX]
+    scratch += [pltpu.VMEM((3, n + 2, 3) + tile, f32) for n in NX]
     scratch += [
-        pltpu.VMEM((3, 2, 3) + tile, f32),
+        pltpu.VMEM((4, 2, 3) + tile, f32),
         pltpu.VMEM((2,) + tile, f32),
         pltpu.VMEM((2, 3) + tile, f32),
         pltpu.SemaphoreType.DMA((4,)),
@@ -878,17 +1031,32 @@
         pltpu.VMEM((2, 2, 2, 3) + tile, f32),
         pltpu.VMEM((2, 3) + tile, f32),
         pltpu.VMEM((2, 2, 3) + tile, f32),
-        pltpu.VMEM((4, 4, nz), f32),
-        pltpu.VMEM((2, 4, 4, nz), f32),
+        pltpu.VMEM((4, 2 * ROWS, nz), f32),
+        pltpu.VMEM((2, 4, 2 * ROWS, nz), f32),
         pltpu.SemaphoreType.DMA((8,)),
         pltpu.SemaphoreType.DMA((2, 8)),
         pltpu.VMEM((4, 14) + tile, f32),
         pltpu.VMEM((2, 14) + tile, f32),
         pltpu.VMEM((2, 7) + tile, f32),
         pltpu.VMEM((2, 7) + tile, f32),
-        pltpu.SemaphoreType.DMA((4,)),
-        pltpu.SemaphoreType.DMA((4,)),
+        pltpu.SemaphoreType.DMA((8,)),
+        pltpu.SemaphoreType.DMA((8,)),
         pltpu.VMEM((NX[0], 3) + tile, f32),
+        pltpu.VMEM((4, 2 * ROWS, nz), f32),
+        pltpu.VMEM((4, 2 * ROWS, nz), f32),
+        pltpu.VMEM((4, 18) + tile, f32),
+        pltpu.VMEM((4, 9) + tile, f32),
+        pltpu.VMEM((4, 3) + tile, f32),
+        pltpu.VMEM((4, 9) + tile, f32),
+        pltpu.VMEM((4, 3) + tile, f32),
+        pltpu.VMEM((2,) + tile, f32),
+        pltpu.VMEM((4, 1, nz), f32),
+        pltpu.VMEM((4, 1, nz), f32),
+        pltpu.VMEM((NX[0], 3) + tile, f32),
+        pltpu.VMEM((2, 13) + tile, f32),
+        pltpu.VMEM((2, 13) + tile, f32),
+        pltpu.SemaphoreType.DMA((12,)),
+        pltpu.SemaphoreType.DMA((12,)),
         pltpu.VMEM(gradient.shape, f32),
         pltpu.VMEM((10,) + tile, f32),
         pltpu.VMEM(coupling.shape, f32),

time: 70.3 us -> 68.9 us (0.980)
  Pallas kernels: 68.6 us -> 67.2 us
    pallas_call x1, Pallas kernels: 68.6 us -> 67.2 us  [local(): pl.pallas_call(functools.partial(kernel, counts), out_shape=jax.ShapeDtyp...]
where the time goes in v6:
time: 68.9 us; the launch traced here: 68.8 us
  Pallas kernels  67.2 us (98%)
  local copies, waits for them, and re-layouts  1.62 us (2%)
    pallas_call x1, Pallas kernels, local(): pl.pallas_call(functools.partial(kernel, counts), out_shape=jax.ShapeDtyp...  67.2 us
    unnamed x1, local copies, waits for them, and re-layouts  1.62 us

profile of v6, /device:TPU:1, one launch (start us, length us, event | category | flops | bytes accessed | tf_op | source)
XLA Modules:
  0.0 68.8 jit_solution(11321468562650844252)
XLA Ops:
  0.0 67.2 %shard_map.64 = f32[3,8,8,256]{3,2,1,0:T(8,128)} custom-call(f32[3,8,8,256]{3,2,1,0:T(8,128)} %grad_in.1, f32[8,8,256]{2,1,0:T(8,128)} %pot_in.1, f32[3,3,8,8,256]{4,3,2,1,0:T(8,128)} %coup_in.1, s32[8,8,256]{2,1,0:T(8,128)} %region_in.1, s32[8,8,256]{2,1,0:T(8,128)} %contact_in.1, f32[4,3]{1,0:T(4,128)} %rates_in.1), custom_call_target="tpu_custom_call" | custom-call | tf_op jit(solution)/shard_map/pallas_call | solution.py:1069
  67.2 1.6 %copy.8 = f32[3,8,8,256]{3,2,1,0:T(8,128)} copy(f32[3,8,8,256]{3,2,1,0:T(8,128)} %shard_map.64) | data formatting | bytes 393216

commit v7 on v6

--- a/solution.py
+++ b/solution.py
@@ -87,7 +87,7 @@
     pair_own, pair_x, pair_y_send, pair_y, pair_corner_send, pair_corner, pair_send_sem, pair_recv_sem = scratch[60:68]
     coef_own, coef_x, coef_y_send, coef_y, coef_send_sem, coef_recv_sem, part, coef_corner_send, coef_corner = scratch[68:77]
     rim_w, rim_r, rim_diag, rim_inverse, rim_base, rim_pot, rim_pot_corner_send, rim_pot_corner = scratch[77:85]
-    base, rim_y_send, rim_y, rim_send_sem, rim_recv_sem = scratch[85:]
+    base, rim_y_send, rim_y, rim_send_sem, rim_recv_sem, result, out_sem = scratch[85:]
     n_x, n_y = counts
     lanes = out.shape[-1]
     gx, gy = lax.axis_index("gx"), lax.axis_index("gy")
@@ -173,21 +173,18 @@
     for name in ("rates", "region", "contact", "coup"):
         loads[name].wait()
 
-    def put_faces(x, first, near):
-        here = pot[x + 1]
-        for k, value in enumerate(near):
-            plus, minus = face_weights(here - value)
-            weights[0][x, 3 * (first + k)] = jnp.ones(tile, jnp.float32)
-            weights[0][x, 3 * (first + k) + 1] = plus
-            weights[0][x, 3 * (first + k) + 2] = minus
+    def put_faces(x, k, plus, minus):
+        weights[0][x, 3 * k] = jnp.ones(tile, jnp.float32)
+        weights[0][x, 3 * k + 1] = plus
+        weights[0][x, 3 * k + 2] = minus
 
     def set_up(x):
         here = pot[x + 1]
-        near = (
-            jnp.where(lane_at == lanes - 1, 0.0, along(here, -1)),
-            jnp.where(lane_at == 0, 0.0, along(here, 1)),
-        )
-        put_faces(x, 4, near)
+        put_faces(x, 4, *face_weights(here - jnp.where(lane_at == lanes - 1, 0.0, along(here, -1))))
+        put_faces(x, 5, *face_weights(here - jnp.where(lane_at == 0, 0.0, along(here, 1))))
+        plus, minus = face_weights(here - down(here, -1))
+        put_faces(x, 2, plus, minus)
+        put_faces(x, 3, down(minus, 1), down(plus, 1))
         at_contact = STRENGTH * contact[x].astype(jnp.float32)
         regions = region[x]
         for c in range(3):
@@ -199,6 +196,10 @@
                 reaction[0][x, 3 * c + d] = value + (extra + at_contact) if c == d else value
 
     each(NX[0], set_up)
+    for x in range(7):
+        plus, minus = face_weights(pot[x + 1] - pot[x + 2])
+        put_faces(x, 0, plus, minus)
+        put_faces(x + 1, 1, minus, plus)
     wait()
     is_low_x, is_high_x = gx == 0, gx == n_x - 1
     is_low_y, is_high_y = gy == 0, gy == n_y - 1
@@ -207,17 +208,14 @@
     pot_y[0] = jnp.where(is_low_y, 0.0, pot_y[0])
     pot_y[1] = jnp.where(is_high_y, 0.0, pot_y[1])
 
-    def cross_faces(x):
-        here = pot[x + 1]
-        near = (
-            pot[x + 2],
-            pot[x],
-            jnp.where(row_at == ROWS - 1, wide(pot_y[1, pl.ds(x, 1), :]), down(here, -1)),
-            jnp.where(row_at == 0, wide(pot_y[0, pl.ds(x, 1), :]), down(here, 1)),
-        )
-        put_faces(x, 0, near)
-
-    each(NX[0], cross_faces)
+    put_faces(0, 1, *face_weights(pot[1] - pot[0]))
+    put_faces(7, 0, *face_weights(pot[8] - pot[9]))
+    for side, k, row in ((0, 2, ROWS - 1), (1, 3, 0)):
+        part[side, 0], part[side, 1] = face_weights(send_y[side, 0] - pot_y[1 - side])
+        for x in range(8):
+            for c in (1, 2):
+                value = wide(part[side, c - 1, x : x + 1, :])
+                weights[0][x, 3 * k + c] = jnp.where(row_at == row, value, weights[0][x, 3 * k + c])
 
     def finish(w, r, diagonal, inv, count):
         def body(x):
@@ -389,12 +387,6 @@
             for c in range(3):
                 w[0, 3 * k + c] = jnp.where(offs[k], 0.0, w[0, 3 * k + c])
 
-    def spread(value, t):
-        value = jnp.where(slot_at == t, value, 0.0)
-        for bit in (1, 2, 4):
-            value = value + along(value, -bit if t & bit else bit)
-        return value
-
     def wide_residual(p, u):
         left = []
         for c in range(3):
@@ -466,7 +458,7 @@
         u = apply_inverse(inverse[LEVELS - 1], 0, b)
         for _ in range(2):
             u = window_sweep(b, u)
-        row = slot_row([spread(value, RADIUS) for value in u + b])
+        row = slot_row([along(value, i - RADIUS) for i, value in enumerate(u + b)])
         low_cell[0] = row[RADIUS : RADIUS + 1, :]
         wait = gather(THIRD, lambda o: low_cell.at[0], low_cells.at[turn], q_send, q_recv.at[turn])
         beside_q()
@@ -887,14 +879,20 @@
         return u, left
 
     def sweep(at, slot, left_of, last=False):
+        copies = []
         for x in range(NX[0]):
             u, left = left_of(0, at, slot, x)
             step = solve(0, x, left)
             for c in range(3):
                 if last:
-                    out[c, x] = u[c] + step[c]
+                    result[c, x] = u[c] + step[c]
                 else:
                     fields[0][at + 1, x + 1, c] = u[c] + step[c]
+            if last:
+                copies.append(pltpu.make_async_copy(result.at[:, x], out.at[:, x], out_sem.at[x]))
+                copies[-1].start()
+        for copy in copies:
+            copy.wait()
         return at + 1
 
     def restrict(level, at, slot, keep=False):
@@ -954,12 +952,15 @@
 
     def beside_second():
         pair_up()
-        ring_pending.extend(send_ring_coefficients())
         mask_level(1)
         finish_level(2)
         coarsen(2)
         pending.append(send_low_coefficients())
+
+    def beside_third():
+        ring_pending.extend(send_ring_coefficients())
         rim_pending.extend(send_rim())
+        take_coefficients(pending)
 
     def beside_fourth():
         take_ring_coefficients(ring_pending)
@@ -972,7 +973,7 @@
         (
             beside_first,
             beside_second,
-            lambda: take_coefficients(pending),
+            beside_third,
             beside_fourth,
         ),
     )
@@ -1058,6 +1059,8 @@
         pltpu.SemaphoreType.DMA((12,)),
         pltpu.SemaphoreType.DMA((12,)),
         pltpu.VMEM(gradient.shape, f32),
+        pltpu.SemaphoreType.DMA((NX[0],)),
+        pltpu.VMEM(gradient.shape, f32),
         pltpu.VMEM((10,) + tile, f32),
         pltpu.VMEM(coupling.shape, f32),
         pltpu.VMEM(region.shape, jnp.int32),
@@ -1065,12 +1068,11 @@
         pltpu.SMEM(rates.shape, f32),
         pltpu.SemaphoreType.DMA((6,)),
     ]
-    vmem = pl.BlockSpec(memory_space=pltpu.VMEM)
     return pl.pallas_call(
         functools.partial(kernel, counts),
         out_shape=jax.ShapeDtypeStruct(gradient.shape, f32),
         in_specs=[pl.BlockSpec(memory_space=pltpu.HBM)] * 6,
-        out_specs=vmem,
+        out_specs=pl.BlockSpec(memory_space=pltpu.HBM),
         scratch_shapes=scratch,
         compiler_params=pltpu.CompilerParams(
             collective_id=0, has_side_effects=True, vmem_limit_bytes=60 * 1024 * 1024

time: 68.9 us -> 65.6 us (0.952)
  Pallas kernels: 67.2 us -> 63.9 us
    pallas_call x1, Pallas kernels: 67.2 us -> 63.9 us  [local(): pl.pallas_call(functools.partial(kernel, counts), out_shape=jax.ShapeDtyp...]
where the time goes in v7:
time: 65.6 us; the launch traced here: 65.5 us
  Pallas kernels  63.9 us (97%)
  local copies, waits for them, and re-layouts  1.62 us (2%)
    pallas_call x1, Pallas kernels, local(): pl.pallas_call(functools.partial(kernel, counts), out_shape=jax.ShapeDtyp...  63.9 us
    unnamed x1, local copies, waits for them, and re-layouts  1.62 us

profile of v7, /device:TPU:1, one launch (start us, length us, event | category | flops | bytes accessed | tf_op | source)
XLA Modules:
  0.0 65.5 jit_solution(8969026121347719197)
XLA Ops:
  0.0 63.9 %shard_map.64 = f32[3,8,8,256]{3,2,1,0:T(8,128)} custom-call(f32[3,8,8,256]{3,2,1,0:T(8,128)} %grad_in.1, f32[8,8,256]{2,1,0:T(8,128)} %pot_in.1, f32[3,3,8,8,256]{4,3,2,1,0:T(8,128)} %coup_in.1, s32[8,8,256]{2,1,0:T(8,128)} %region_in.1, s32[8,8,256]{2,1,0:T(8,128)} %contact_in.1, f32[4,3]{1,0:T(4,128)} %rates_in.1), custom_call_target="tpu_custom_call" | custom-call | tf_op jit(solution)/shard_map/pallas_call | solution.py:1071
  63.9 1.6 %copy.8 = f32[3,8,8,256]{3,2,1,0:T(8,128)} copy(f32[3,8,8,256]{3,2,1,0:T(8,128)} %shard_map.64) | data formatting | bytes 393216

commit v8 on v7

--- a/solution.py
+++ b/solution.py
@@ -87,7 +87,9 @@
     pair_own, pair_x, pair_y_send, pair_y, pair_corner_send, pair_corner, pair_send_sem, pair_recv_sem = scratch[60:68]
     coef_own, coef_x, coef_y_send, coef_y, coef_send_sem, coef_recv_sem, part, coef_corner_send, coef_corner = scratch[68:77]
     rim_w, rim_r, rim_diag, rim_inverse, rim_base, rim_pot, rim_pot_corner_send, rim_pot_corner = scratch[77:85]
-    base, rim_y_send, rim_y, rim_send_sem, rim_recv_sem, result, out_sem = scratch[85:]
+    base, rim_y_send, rim_y, rim_send_sem, rim_recv_sem, result, out_sem = scratch[85:92]
+    halo_inverse, cross, cross_send, cross_recv, lean, lean_x, lean_y_send, lean_y = scratch[92:100]
+    lean_send_sem, lean_recv_sem = scratch[100:]
     n_x, n_y = counts
     lanes = out.shape[-1]
     gx, gy = lax.axis_index("gx"), lax.axis_index("gy")
@@ -801,7 +803,7 @@
         v = inverse[level]
         return [v[x, 3 * c] * r[0] + v[x, 3 * c + 1] * r[1] + v[x, 3 * c + 2] * r[2] for c in range(3)]
 
-    def share(level, at, beside_it=lambda: None):
+    def post(level, at):
         slot, f, count = done[0] % 3, fields[level], NX[level]
         for side, row in ((0, ROWS - 1), (1, 0)):
             for c in range(3):
@@ -817,6 +819,10 @@
                 (send_y.at[1], rows_halo.at[slot, 1]),
             ]
         )
+        return slot, wait
+
+    def share(level, at, beside_it):
+        slot, wait = post(level, at)
         beside_it()
         inner(level, at)
         wait()
@@ -841,13 +847,16 @@
                         value = value - r[x, 3 * d + c] * u[d]
                 part[x, c] = value
 
-    def rest(level, at, slot, x):
+    def rest(level, at, slot, x, stride=1, whole=True):
         f, w, span, count = fields[level], weights[level], 1 << level, NX[level]
         left = []
         for c in range(3):
-            row_high, row_low = (rows_halo[slot, side, c, x : x + 1, :] for side in (1, 0))
+            row = x * stride
+            row_high, row_low = (rows_halo[slot, side, c, row : row + 1, :] for side in (1, 0))
             value = jnp.where(row_at >= ROWS - span, w[x, 6 + c] * wide(row_high), 0.0)
-            value = part[x, c] + jnp.where(row_at < span, w[x, 9 + c] * wide(row_low), value)
+            value = jnp.where(row_at < span, w[x, 9 + c] * wide(row_low), value)
+            if whole:
+                value = part[x, c] + value
             if x == 0:
                 value = value + w[x, 3 + c] * f[at, 0, c]
             if x == count - 1:
@@ -895,12 +904,78 @@
             copy.wait()
         return at + 1
 
-    def restrict(level, at, slot, keep=False):
+    def make_halo_inverse():
+        for i in range(9):
+            for side in range(2):
+                row = 1 + 5 * side
+                halo_inverse[side, i] = doubled([ring_inverse[5 * side, i, 2 + k : 3 + k, :] for k in range(4)])
+                halo_inverse[2 + side, i] = doubled([ring_inverse[1 + k, i, row : row + 1, :] for k in range(4)])
+
+    def restrict_with_halo(at):
+        slot, wait = post(0, at)
+        rows, lanes_ = pair_tools(0)[4:]
+        outside = (is_low_x, is_high_x, is_low_y, is_high_y)
+        for t in range(4):
+            for c in range(3):
+                edge = fields[0][at, 1 + 7 * t, c] if t < 2 else send_y[3 - t, c]
+                value = jnp.where(outside[t], 0.0, rim_w[t, 3 * t + c] * edge)
+                cross[t, c] = lanes_(rows(value))
+        copies = []
+        sems = lambda n: (lean_send_sem.at[n], lean_recv_sem.at[n])
+        for n in range(4):
+            sx, sy = n // 2, n % 2
+            for c in range(3):
+                row = 6 - 6 * sx
+                cross_send[n, c : c + 1, :] = cross[3 - sy, c, row : row + 1, :]
+                row = 6 - 6 * sy
+                cross_send[n, 3 + c : 4 + c, :] = cross[1 - sx, c, row : row + 1, :]
+            copies.append(remote(cross_send.at[n], cross_recv.at[n], *sems(4 + n), (1 - 2 * sx, 1 - 2 * sy)))
+        inner(0, at)
+        for x in range(4):
+            for c in range(3):
+                lean[x, c] = lanes_(rows(part[2 * x, c] + part[2 * x + 1, c]))
+        for side, to in ((0, 1), (1, -1)):
+            row = 6 - 6 * side
+            for c in range(3):
+                lean_y_send[side, c] = doubled([lean[k, c, row : row + 1, :] for k in range(4)])
+            copies.append(remote(lean_y_send.at[side], lean_y.at[side], *sems(side), (0, to)))
+            copies.append(remote(lean.at[3 - 3 * side], lean_x.at[side], *sems(2 + side), (to, 0)))
+        wait()
+        for x in range(4):
+            more = [rest(0, at, slot, 2 * x + i, whole=False)[1] for i in range(2)]
+            total = [lean[x, c] + lanes_(rows(more[0][c] + more[1][c])) for c in range(3)]
+            first = solve(1, x, total)
+            for c in range(3):
+                sources[1][x, c] = total[c]
+                fields[1][0, x + 1, c] = first[c]
+        for copy in copies:
+            copy.wait()
+        for t in range(4):
+            side = t % 2
+            total = []
+            for c in range(3):
+                if t < 2:
+                    value, first, last, row = lean_x[side, c], 2 * side, 2 * side + 1, c
+                else:
+                    value, first, last, row = lean_y[side, c], side, 2 + side, 3 + c
+                low, high = (wide(cross_recv[n, row : row + 1, :]) for n in (first, last))
+                value = value + cross[t, c]
+                total.append(value + jnp.where(row_at < 2, low, jnp.where(row_at >= 6, high, 0.0)))
+            first = apply_inverse(halo_inverse, t, total)
+            for c in range(3):
+                if t < 2:
+                    fields[1][0, 5 * side, c] = first[c]
+                else:
+                    rows_halo[3, side, c] = first[c]
+        inner(1, 0)
+        return slot
+
+    def restrict(level, at, slot, keep=False, stride=1):
         rows, lanes_ = pair_tools(level)[4:]
         for x in range(NX[level + 1]):
             left = []
             for i in range(2):
-                u, r = rest(level, at, slot, 2 * x + i)
+                u, r = rest(level, at, slot, 2 * x + i, stride)
                 left.append(r)
                 if keep:
                     step = solve(level, 2 * x + i, r)
@@ -913,21 +988,30 @@
                 fields[level + 1][0, x + 1, c] = first[c]
 
     def cycle(at, turn, besides, last=False):
-        slot = share(0, at, besides[0])
-        restrict(0, at, slot, keep=not last)
         pairs = []
-
-        def beside():
-            pairs.extend(send_pairs(turn))
-            besides[1]()
-
-        restrict(1, 0, share(1, 0, beside))
+        if last:
+            slot = restrict_with_halo(at)
+            restrict(1, 0, 3, stride=2)
+        else:
+            slot = share(0, at, besides[0])
+            restrict(0, at, slot, keep=True)
+
+            def beside():
+                pairs.extend(send_pairs(turn))
+                besides[1]()
+
+            restrict(1, 0, share(1, 0, beside))
+
+        def beside_p():
+            if last:
+                pairs.extend(send_pairs(turn))
+            besides[2]()
 
         def beside_q():
             take_pairs(turn, pairs)
             besides[3]()
 
-        lower(turn, besides[2], beside_q)
+        lower(turn, beside_p, beside_q)
         ring_sweep()
         if not last:
             rim_sweep(at + 1)
@@ -965,6 +1049,7 @@
     def beside_fourth():
         take_ring_coefficients(ring_pending)
         take_rim(rim_pending)
+        make_halo_inverse()
 
     nothing = lambda: None
     at = cycle(
@@ -1060,6 +1145,16 @@
         pltpu.SemaphoreType.DMA((12,)),
         pltpu.VMEM(gradient.shape, f32),
         pltpu.SemaphoreType.DMA((NX[0],)),
+        pltpu.VMEM((4, 9) + tile, f32),
+        pltpu.VMEM((4, 3) + tile, f32),
+        pltpu.VMEM((4,) + tile, f32),
+        pltpu.VMEM((4,) + tile, f32),
+        pltpu.VMEM((4, 3) + tile, f32),
+        pltpu.VMEM((2, 3) + tile, f32),
+        pltpu.VMEM((2, 3) + tile, f32),
+        pltpu.VMEM((2, 3) + tile, f32),
+        pltpu.SemaphoreType.DMA((8,)),
+        pltpu.SemaphoreType.DMA((8,)),
         pltpu.VMEM(gradient.shape, f32),
         pltpu.VMEM((10,) + tile, f32),
         pltpu.VMEM(coupling.shape, f32),

time: 65.6 us -> 61.1 us (0.931)
  Pallas kernels: 63.9 us -> 59.3 us
    pallas_call x1, Pallas kernels: 63.9 us -> 59.3 us  [local(): pl.pallas_call(functools.partial(kernel, counts), out_shape=jax.ShapeDtyp...]
where the time goes in v8:
time: 61.1 us; the launch traced here: 61 us
  Pallas kernels  59.3 us (97%)
  local copies, waits for them, and re-layouts  1.62 us (3%)
    pallas_call x1, Pallas kernels, local(): pl.pallas_call(functools.partial(kernel, counts), out_shape=jax.ShapeDtyp...  59.3 us
    unnamed x1, local copies, waits for them, and re-layouts  1.62 us

profile of v8, /device:TPU:1, one launch (start us, length us, event | category | flops | bytes accessed | tf_op | source)
XLA Modules:
  0.0 61.0 jit_solution(16959837618076268945)
XLA Ops:
  0.0 59.3 %shard_map.64 = f32[3,8,8,256]{3,2,1,0:T(8,128)} custom-call(f32[3,8,8,256]{3,2,1,0:T(8,128)} %grad_in.1, f32[8,8,256]{2,1,0:T(8,128)} %pot_in.1, f32[3,3,8,8,256]{4,3,2,1,0:T(8,128)} %coup_in.1, s32[8,8,256]{2,1,0:T(8,128)} %region_in.1, s32[8,8,256]{2,1,0:T(8,128)} %contact_in.1, f32[4,3]{1,0:T(4,128)} %rates_in.1), custom_call_target="tpu_custom_call" | custom-call | tf_op jit(solution)/shard_map/pallas_call | solution.py:1166
  59.3 1.6 %copy.8 = f32[3,8,8,256]{3,2,1,0:T(8,128)} copy(f32[3,8,8,256]{3,2,1,0:T(8,128)} %shard_map.64) | data formatting | bytes 393216

commit v9 on v8

--- a/solution.py
+++ b/solution.py
@@ -89,7 +89,7 @@
     rim_w, rim_r, rim_diag, rim_inverse, rim_base, rim_pot, rim_pot_corner_send, rim_pot_corner = scratch[77:85]
     base, rim_y_send, rim_y, rim_send_sem, rim_recv_sem, result, out_sem = scratch[85:92]
     halo_inverse, cross, cross_send, cross_recv, lean, lean_x, lean_y_send, lean_y = scratch[92:100]
-    lean_send_sem, lean_recv_sem = scratch[100:]
+    lean_send_sem, lean_recv_sem, r_wide_2 = scratch[100:]
     n_x, n_y = counts
     lanes = out.shape[-1]
     gx, gy = lax.axis_index("gx"), lax.axis_index("gy")
@@ -389,16 +389,19 @@
             for c in range(3):
                 w[0, 3 * k + c] = jnp.where(offs[k], 0.0, w[0, 3 * k + c])
 
-    def wide_residual(p, u):
+    def turned(u, k):
+        turn = -1 if k % 2 == 0 else 1
+        return down(u, turn) if k < 2 else along(u, turn if k < 4 else turn * SLOTS)
+
+    def wide_residual(p, u, b, near_of):
         left = []
         for c in range(3):
-            value = b_wide[p, c] - diag_wide[p, c] * u[p][c]
+            value = -diag_wide[p, c] * u[p][c]
+            if b is not None:
+                value = b[p, c] + value
             for k in range(6):
-                bit, ahead = bits[k], k % 2 == 0
-                near = u[p ^ bit][c]
-                if ((p & bit) != 0) == ahead:
-                    turn = -1 if ahead else 1
-                    near = down(near, turn) if k < 2 else along(near, turn if k < 4 else turn * SLOTS)
+                bit = bits[k]
+                near = near_of(p ^ bit, c, k) if ((p & bit) != 0) == (k % 2 == 0) else u[p ^ bit][c]
                 value = value + w_wide[p, 3 * k + c] * near
             for d in range(3):
                 if d != c:
@@ -455,8 +458,10 @@
         u_mid = wide_fields()
         b = [jnp.zeros(tile, jnp.float32) for _ in range(3)]
         for p in range(SLOTS):
-            left = wide_residual(p, u_mid)
-            b = [b[c] + left[c] for c in range(3)]
+            left = wide_residual(p, u_mid, b_wide, lambda q, c, k: turned(u_mid[q][c], k))
+            for c in range(3):
+                b[c] = b[c] + left[c]
+                r_wide_2[p, c] = left[c]
         u = apply_inverse(inverse[LEVELS - 1], 0, b)
         for _ in range(2):
             u = window_sweep(b, u)
@@ -464,6 +469,10 @@
         low_cell[0] = row[RADIUS : RADIUS + 1, :]
         wait = gather(THIRD, lambda o: low_cell.at[0], low_cells.at[turn], q_send, q_recv.at[turn])
         beside_q()
+        for p in range(SLOTS):
+            step = apply_inverse(inverse_wide, p, [r_wide_2[p, c] for c in range(3)])
+            for c in range(3):
+                u_wide[p, c] += step[c]
         wait()
         made = unpacked(THIRD, lambda n: low_cells[turn, n], low_cell[0])
         u, b = made[:3], made[3:6]
@@ -480,11 +489,12 @@
         u = window_sweep(b, u, (before_x, before_y))
         for _ in range(COARSE_SWEEPS - 4):
             u = window_sweep(b, u)
-        u_mid = [[u_wide[p, c] + u[c] for c in range(3)] for p in range(SLOTS)]
+        around_e = [[turned(u[c], k) for k in range(6)] for c in range(3)]
         last = []
         for p in range(SLOTS):
-            step = apply_inverse(inverse_wide, p, wide_residual(p, u_mid))
-            last.append([u_mid[p][c] + step[c] for c in range(3)])
+            left = wide_residual(p, [u] * SLOTS, None, lambda q, c, k: around_e[c][k])
+            step = apply_inverse(inverse_wide, p, left)
+            last.append([u_wide[p, c] + u[c] + step[c] for c in range(3)])
         for c in range(3):
             for x in range(2):
                 for at, (t, y) in enumerate(((RADIUS - 1, 1), (RADIUS, 0), (RADIUS, 1), (RADIUS + 1, 0))):
@@ -653,21 +663,6 @@
             step = apply_inverse(ring_inverse, p, left)
             for c in range(3):
                 ring_out[p, c] = u[c] + step[c]
-
-    def add_to_finest(at, slot):
-        f = fields[0]
-        for c in range(3):
-            for p in range(6):
-                rows = [wide(ring_out[p, c, 2 + k : 3 + k, :]) for k in range(4)]
-                e = jnp.where(row_at < 2, rows[0], rows[1])
-                e = jnp.where(row_at < 4, e, jnp.where(row_at < 6, rows[2], rows[3]))
-                for x in {0: (-1,), 5: (8,)}.get(p, (2 * p - 2, 2 * p - 1)):
-                    f[at, x + 1, c] += e
-            for side, row in ((0, 1), (1, 6)):
-                rows = [wide(ring_out[1 + k, c, row : row + 1, :]) for k in range(4)]
-                e = jnp.where(row_at < 2, rows[0], rows[1])
-                e = jnp.where(row_at < 4, e, jnp.where(row_at < 6, rows[2], rows[3]))
-                rows_halo[slot, side, c] += e
 
     def packed_y(f, at):
         return rows_tile([(x, f(x)[at : at + 1, :]) for x in range(8)])
@@ -887,21 +882,12 @@
             left.append(value)
         return u, left
 
-    def sweep(at, slot, left_of, last=False):
-        copies = []
+    def sweep(at, slot, left_of):
         for x in range(NX[0]):
             u, left = left_of(0, at, slot, x)
             step = solve(0, x, left)
             for c in range(3):
-                if last:
-                    result[c, x] = u[c] + step[c]
-                else:
-                    fields[0][at + 1, x + 1, c] = u[c] + step[c]
-            if last:
-                copies.append(pltpu.make_async_copy(result.at[:, x], out.at[:, x], out_sem.at[x]))
-                copies[-1].start()
-        for copy in copies:
-            copy.wait()
+                fields[0][at + 1, x + 1, c] = u[c] + step[c]
         return at + 1
 
     def make_halo_inverse():
@@ -943,6 +929,9 @@
         wait()
         for x in range(4):
             more = [rest(0, at, slot, 2 * x + i, whole=False)[1] for i in range(2)]
+            for i in range(2):
+                for c in range(3):
+                    base[2 * x + i, c] = part[2 * x + i, c] + more[i][c]
             total = [lean[x, c] + lanes_(rows(more[0][c] + more[1][c])) for c in range(3)]
             first = solve(1, x, total)
             for c in range(3):
@@ -978,14 +967,62 @@
                 u, r = rest(level, at, slot, 2 * x + i, stride)
                 left.append(r)
                 if keep:
-                    step = solve(level, 2 * x + i, r)
                     for c in range(3):
-                        base[2 * x + i, c] = u[c] + step[c]
+                        base[2 * x + i, c] = r[c]
             total = [lanes_(rows(left[0][c] + left[1][c])) for c in range(3)]
             first = solve(level + 1, x, total)
             for c in range(3):
                 sources[level + 1][x, c] = total[c]
                 fields[level + 1][0, x + 1, c] = first[c]
+
+    def make_base(at):
+        for x in range(NX[0]):
+            step = solve(0, x, [base[x, c] for c in range(3)])
+            for c in range(3):
+                base[x, c] = fields[0][at, x + 1, c] + step[c]
+
+    def correct_finest(at, last):
+        copies = []
+        planes = [[doubled([ring_out[p, c, 2 + k : 3 + k, :] for k in range(4)]) for c in range(3)] for p in range(6)]
+        w, r, v = weights[0], reaction[0], inverse[0]
+        for p in range(1, 5):
+            e = planes[p]
+            turned = []
+            for c in range(3):
+                after, before = wide(ring_out[p, c, 6:7, :]), wide(ring_out[p, c, 1:2, :])
+                turned.append(
+                    (
+                        jnp.where(row_at == ROWS - 1, after, down(e[c], -1)),
+                        jnp.where(row_at == 0, before, down(e[c], 1)),
+                        along(e[c], -1),
+                        along(e[c], 1),
+                    )
+                )
+            for i in range(2):
+                x = 2 * p - 2 + i
+                left = []
+                for c in range(3):
+                    near = (e[c] if i == 0 else planes[p + 1][c], planes[p - 1][c] if i == 0 else e[c]) + turned[c]
+                    value = -diag[0][x, c] * e[c]
+                    for k in range(6):
+                        value = value + w[x, 3 * k + c] * near[k]
+                    for d in range(3):
+                        if d != c:
+                            value = value - r[x, 3 * d + c] * e[d]
+                    left.append(value)
+                step = apply_inverse(v, x, left)
+                for c in range(3):
+                    value = base[x, c] + e[c] + step[c]
+                    if last:
+                        result[c, x] = value
+                    else:
+                        fields[0][at + 1, x + 1, c] = value
+                if last:
+                    copies.append(pltpu.make_async_copy(result.at[:, x], out.at[:, x], out_sem.at[x]))
+                    copies[-1].start()
+        for copy in copies:
+            copy.wait()
+        return at + 1
 
     def cycle(at, turn, besides, last=False):
         pairs = []
@@ -999,12 +1036,14 @@
             def beside():
                 pairs.extend(send_pairs(turn))
                 besides[1]()
+                make_base(at)
 
             restrict(1, 0, share(1, 0, beside))
 
         def beside_p():
             if last:
                 pairs.extend(send_pairs(turn))
+                make_base(at)
             besides[2]()
 
         def beside_q():
@@ -1015,8 +1054,7 @@
         ring_sweep()
         if not last:
             rim_sweep(at + 1)
-        add_to_finest(at, slot)
-        return sweep(at, slot, residual, last)
+        return correct_finest(at, last)
 
     def start(x):
         for c, value in enumerate(solve(0, x, source(0, x))):
@@ -1155,6 +1193,7 @@
         pltpu.VMEM((2, 3) + tile, f32),
         pltpu.SemaphoreType.DMA((8,)),
         pltpu.SemaphoreType.DMA((8,)),
+        pltpu.VMEM((SLOTS, 3) + tile, f32),
         pltpu.VMEM(gradient.shape, f32),
         pltpu.VMEM((10,) + tile, f32),
         pltpu.VMEM(coupling.shape, f32),

time: 61.1 us -> 60.9 us (level)
  no operation moved by 1% of the time
where the time goes in v9:
time: 60.9 us; the launch traced here: 60.8 us
  Pallas kernels  59.1 us (97%)
  local copies, waits for them, and re-layouts  1.62 us (3%)
    pallas_call x1, Pallas kernels, local(): pl.pallas_call(functools.partial(kernel, counts), out_shape=jax.ShapeDtyp...  59.1 us
    unnamed x1, local copies, waits for them, and re-layouts  1.62 us

profile of v9, /device:TPU:1, one launch (start us, length us, event | category | flops | bytes accessed | tf_op | source)
XLA Modules:
  0.0 60.8 jit_solution(6627392167412053470)
XLA Ops:
  0.0 59.1 %shard_map.64 = f32[3,8,8,256]{3,2,1,0:T(8,128)} custom-call(f32[3,8,8,256]{3,2,1,0:T(8,128)} %grad_in.1, f32[8,8,256]{2,1,0:T(8,128)} %pot_in.1, f32[3,3,8,8,256]{4,3,2,1,0:T(8,128)} %coup_in.1, s32[8,8,256]{2,1,0:T(8,128)} %region_in.1, s32[8,8,256]{2,1,0:T(8,128)} %contact_in.1, f32[4,3]{1,0:T(4,128)} %rates_in.1), custom_call_target="tpu_custom_call" | custom-call | tf_op jit(solution)/shard_map/pallas_call | solution.py:1205
  59.1 1.6 %copy.8 = f32[3,8,8,256]{3,2,1,0:T(8,128)} copy(f32[3,8,8,256]{3,2,1,0:T(8,128)} %shard_map.64) | data formatting | bytes 393216

commit v10 on v9

--- a/solution.py
+++ b/solution.py
@@ -19,11 +19,16 @@
 SLOTS = 8
 
 
+def by_links(offsets):
+    along_x, along_y = (0, 1, 1, 2, 2, 3, 3), (0, 2, 3, 2, 1, 2, 3)
+    return sorted(offsets, key=lambda o: (-along_x[abs(o[0])] - along_y[abs(o[1])], o))
+
+
 def around(shape, far):
     reach = range(-6, 7)
     distance = lambda i, j: min(abs(i - a) + abs(j - b) for a, b in shape)
     found = [(i, j) for i in reach for j in reach if distance(i, j) <= far and (i, j) != (0, 0)]
-    return sorted(found, key=lambda o: -abs(o[0]) - abs(o[1]))
+    return by_links(found)
 
 
 OWN = [(0, 0)]
@@ -439,7 +444,7 @@
         for c in range(3):
             mid_cell[0, c] = child_row(sources[2], 0, c)
             mid_cell[1, c] = child_row(fields[2].at[0], 1, c)
-        near = INNER + OUTER
+        near = by_links(INNER + OUTER)
         wait = gather(
             near, lambda o: mid_cell.at[0 if o in INNER else 1], mid_cells.at[turn], p_send, p_recv.at[turn]
         )

time: 60.9 us -> 60.6 us (level)
  no operation moved by 1% of the time
where the time goes in v10:
time: 60.6 us; the launch traced here: 60.5 us
  Pallas kernels  58.9 us (97%)
  local copies, waits for them, and re-layouts  1.62 us (3%)
    pallas_call x1, Pallas kernels, local(): pl.pallas_call(functools.partial(kernel, counts), out_shape=jax.ShapeDtyp...  58.9 us
    unnamed x1, local copies, waits for them, and re-layouts  1.62 us

profile of v10, /device:TPU:1, one launch (start us, length us, event | category | flops | bytes accessed | tf_op | source)
XLA Modules:
  0.0 60.5 jit_solution(14628482017176355077)
XLA Ops:
  0.0 58.9 %shard_map.64 = f32[3,8,8,256]{3,2,1,0:T(8,128)} custom-call(f32[3,8,8,256]{3,2,1,0:T(8,128)} %grad_in.1, f32[8,8,256]{2,1,0:T(8,128)} %pot_in.1, f32[3,3,8,8,256]{4,3,2,1,0:T(8,128)} %coup_in.1, s32[8,8,256]{2,1,0:T(8,128)} %region_in.1, s32[8,8,256]{2,1,0:T(8,128)} %contact_in.1, f32[4,3]{1,0:T(4,128)} %rates_in.1), custom_call_target="tpu_custom_call" | custom-call | tf_op jit(solution)/shard_map/pallas_call | solution.py:1210
  58.9 1.6 %copy.8 = f32[3,8,8,256]{3,2,1,0:T(8,128)} copy(f32[3,8,8,256]{3,2,1,0:T(8,128)} %shard_map.64) | data formatting | bytes 393216
